TPU v7x, 256 devices: a whole 4x4x8 slice. The times are simulated.
256 devices in a mesh: tile: 16 (over z, core), lev: 4 (over x), tag: 4 (over y).
Axes of the slice: x: 4, y: 4, z: 8, core: 2. Of those that a mesh axis runs over, the one named last changes fastest.
Arguments:
- parent_field: float32 [8, 32, 256, 1024], P('tag', 'lev', 'tile'), may hold values from -6 to 6
- nest_field: float32 [8, 32, 256, 1024], P('tag', 'lev', 'tile'), may hold values from -6 to 6
- parent_mixing: float32 [32, 256, 1024], P('lev', 'tile'), may hold values from 0.05 to 5
- parent_eastward: float32 [256, 1024], P('tile'), may hold values from 0.02 to 0.12
- parent_northward: float32 [256, 1024], P('tile'), may hold values from 0.02 to 0.12
- nest_eastward: float32 [256, 1024], P('tile'), may hold values from 0.02 to 0.12
- nest_northward: float32 [256, 1024], P('tile'), may hold values from 0.02 to 0.12
- strip_tile: int32 [16, 256], replicated, may hold values from 0 to 15, as said below
- strip_block: int32 [16, 256], replicated, may hold values from 0 to 127
- strip_target: int32 [16, 256], replicated, may hold values from 0 to 127
- strip_count: int32 [16], replicated, may hold values from 1 to 256, as said below
Outputs:
- parent_adjoint: float32 [8, 32, 256, 1024], P('tag', 'lev', 'tile')
- nest_adjoint: float32 [8, 32, 256, 1024], P('tag', 'lev', 'tile')
- bulk_adjoint: float32 [32, 256, 1024], P('lev', 'tile', 'tag')
Inputs may be any that keep to these rules, and one draw needn't show every extreme that they name: `strip_tile`: among the first strip_count[j] entries of row j, every parent tile appears at most 16 times; in the row whose count is 256 every parent tile appears exactly 16 times. `strip_count`: exactly one nest tile lists 256 strips; every other lists at most 128.
All inputs are finite; a program needn't handle non-finite values.
Results may differ from a plain program's by a relative error of at most 0.0003.
Values sent between devices are 32-bit elements; how exact they have to be, the bound alone decides.
A program may use at most 64 MiB of HBM per device.

v0:
```python
import jax
import jax.numpy as jnp
from jax import lax
from jax.sharding import PartitionSpec as P

CAP = 16
NSUB = 3


HIGHEST = lax.Precision.HIGHEST


def extended(cells, sides, width):
    for axis, dim in sides:
        count = lax.axis_size(axis)
        ends = count - 1
        head = lax.slice_in_dim(cells, 0, width, axis=dim)
        tail = lax.slice_in_dim(cells, cells.shape[dim] - width, cells.shape[dim], axis=dim)
        cells = jnp.concatenate(
            [
                lax.ppermute(tail, axis, [(i, (i + 1) % count) for i in range(ends)]),
                cells,
                lax.ppermute(head, axis, [((i + 1) % count, i) for i in range(ends)]),
            ],
            axis=dim,
        )
    return cells


def tridiagonal(source, mixing):
    level_count = mixing.shape[0]
    mixing_up = jnp.concatenate([mixing[1:], jnp.zeros_like(mixing[:1])], axis=0)
    diagonal = 1.0 + mixing + mixing_up
    ratio_now = jnp.zeros_like(mixing[0])
    carry_now = jnp.zeros_like(source[:, 0])
    ratios = []
    carries = []
    for lev_index in range(level_count):
        pivot_now = diagonal[lev_index] + mixing[lev_index] * ratio_now
        ratio_now = -mixing_up[lev_index] / pivot_now
        carry_now = (source[:, lev_index] + mixing[lev_index] * carry_now) / pivot_now
        ratios.append(ratio_now)
        carries.append(carry_now)
    value_now = carries[level_count - 1]
    results = [value_now]
    for lev_index in range(level_count - 2, -1, -1):
        value_now = carries[lev_index] - ratios[lev_index] * value_now
        results.append(value_now)
    return jnp.stack(results[::-1], axis=1)


def relax(padded, eastward):
    center = padded[:-1, 1:-1]
    row_above = padded[:-1, :-2]
    row_below = padded[:-1, 2:]
    north_here = padded[-1, 1:-1]
    north_above = padded[-1, :-2]
    zero_column = jnp.zeros_like(center[:, :, :1])
    east_cell = jnp.concatenate([center[:, :, 1:], zero_column], axis=2)
    west_cell = jnp.concatenate([zero_column, center[:, :, :-1]], axis=2)
    west_rate = jnp.concatenate([jnp.zeros_like(eastward[:, :1]), eastward[:, :-1]], axis=1)
    return (
        center
        + north_here * (row_below - center)
        + north_above * (row_above - center)
        + eastward * (east_cell - center)
        + west_rate * (west_cell - center)
    )


def rims(stacked):
    return extended(stacked, (("tile", 1),), 1)


def advance(start, solved, parent_eastward, parent_northward, nest_eastward, nest_northward):
    tag_count, level_count, row_count, col_count = start.shape
    line_count = tag_count * level_count
    nest_now = start.reshape(line_count, row_count, col_count)
    parent_now = solved.reshape(line_count, row_count, col_count)
    for sub_step in range(NSUB):
        nest_stack = jnp.concatenate([nest_now, nest_northward[None]], axis=0)
        if sub_step == 0:
            parent_stack = jnp.concatenate([parent_now, parent_northward[None]], axis=0)
            padded = rims(jnp.concatenate([parent_stack, nest_stack], axis=0))
            parent_now = relax(padded[: line_count + 1], parent_eastward)
            nest_now = relax(padded[line_count + 1 :], nest_eastward)
        else:
            nest_now = relax(rims(nest_stack), nest_eastward)
    full_shape = (tag_count, level_count, row_count, col_count)
    return (parent_now.reshape(full_shape), nest_now.reshape(full_shape))


def deliver(parent_field, strip_tile, strip_block, strip_target, strip_count):
    tag_count, level_count, row_count, col_count = parent_field.shape
    line_count = tag_count * level_count
    block_count = row_count * col_count // 128
    tile_count, slot_total = strip_tile.shape
    own_index = lax.axis_index("tile")
    positions = jnp.arange(slot_total, dtype=jnp.int32)
    is_live = positions[None, :] < strip_count[:, None]
    from_here = jnp.logical_and(is_live, strip_tile == own_index).astype(jnp.int32)
    slot_rank = jnp.cumsum(from_here, axis=1) - 1
    slot_index = jnp.arange(CAP, dtype=jnp.int32)
    select = from_here[:, None, :] * (slot_rank[:, None, :] == slot_index[None, :, None]).astype(
        jnp.int32
    )
    source_block = jnp.sum(select * strip_block[:, None, :], axis=2).reshape(-1)
    filled = jnp.sum(select, axis=2).reshape(-1).astype(jnp.float32)
    blocks = parent_field.reshape(line_count, block_count, 128)
    packed = jnp.take(blocks, source_block, axis=1) * filled[None, :, None]
    received = lax.all_to_all(packed, "tile", split_axis=1, concat_axis=1, tiled=True)
    own_tile = lax.dynamic_index_in_dim(strip_tile, own_index, 0, keepdims=False)
    own_target = lax.dynamic_index_in_dim(strip_target, own_index, 0, keepdims=False)
    own_count = lax.dynamic_index_in_dim(strip_count, own_index, 0, keepdims=False)
    own_live = (positions < own_count).astype(jnp.int32)
    from_source = (own_tile[:, None] == jnp.arange(tile_count, dtype=jnp.int32)[None, :]).astype(
        jnp.int32
    ) * own_live[:, None]
    own_rank = jnp.sum((jnp.cumsum(from_source, axis=0) - 1) * from_source, axis=1)
    arrival = own_tile * CAP + own_rank
    pick_slot = (arrival[:, None] == jnp.arange(tile_count * CAP, dtype=jnp.int32)[None, :]).astype(
        jnp.float32
    )
    pick_slot = pick_slot * own_live[:, None].astype(jnp.float32)
    place_block = (own_target[:, None] == jnp.arange(block_count, dtype=jnp.int32)[None, :]).astype(
        jnp.float32
    )
    routing = jnp.dot(pick_slot.T, place_block, precision=HIGHEST)
    forcing = jnp.einsum("lic,ib->lbc", received, routing, precision=HIGHEST)
    return forcing.reshape(tag_count, level_count, row_count, col_count)


def shards(
    parent_field,
    nest_field,
    parent_mixing,
    parent_eastward,
    parent_northward,
    nest_eastward,
    nest_northward,
    strip_tile,
    strip_block,
    strip_target,
    strip_count,
):
    tag_count = parent_field.shape[0]
    forcing = deliver(parent_field, strip_tile, strip_block, strip_target, strip_count)
    stacked = jnp.concatenate([parent_field, parent_mixing[None]], axis=0)
    columns = lax.all_to_all(stacked, "lev", split_axis=3, concat_axis=1, tiled=True)
    column_result = tridiagonal(columns[:tag_count], columns[tag_count])
    solved = lax.all_to_all(column_result, "lev", split_axis=1, concat_axis=3, tiled=True)
    parent_adjoint, nest_adjoint = advance(
        nest_field + forcing,
        solved,
        parent_eastward,
        parent_northward,
        nest_eastward,
        nest_northward,
    )
    bulk_adjoint = lax.psum_scatter(
        jnp.sum(parent_adjoint, axis=0), "tag", scatter_dimension=2, tiled=True
    )
    return (parent_adjoint, nest_adjoint, bulk_adjoint)


def solution(mesh):
    in_specs = (
        P("tag", "lev", "tile", None),
        P("tag", "lev", "tile", None),
        P("lev", "tile", None),
        P("tile", None),
        P("tile", None),
        P("tile", None),
        P("tile", None),
        P(),
        P(),
        P(),
        P(),
    )
    out_specs = (
        P("tag", "lev", "tile", None),
        P("tag", "lev", "tile", None),
        P("lev", "tile", "tag"),
    )
    return jax.shard_map(shards, mesh=mesh, in_specs=in_specs, out_specs=out_specs, check_vma=False)
```

profile of v0, /device:TPU:1, one launch (start us, length us, event | category | flops | bytes accessed | tf_op | source)
XLA Modules:
  0.0 209.0 jit_solution(3081090923372214536)
XLA Ops:
  7.2 1.5 pad_maximum_fusion.5
  8.7 6.9 %copy.55 = f32[3,8,16,1024]{2,1,0,3:T(8,128)} copy(f32[3,8,16,1024]{3,2,1,0:T(8,128)S(1)} %pad_maximum_fusion.5) | data formatting | bytes 3145728 | tf_op jit(solution)/shard_map/concatenate | solution.py:148
  15.6 8.3 %reshape.176 = f32[4,1,98304]{2,1,0:T(1,128)} reshape(f32[1024,3,8,16]{3,2,1,0:T(8,128)} %bitcast.230) | data formatting | bytes 3145728
  23.9 5.0 %all-to-all-start = ((f32[4,1,98304]{2,1,0:T(1,128)}), f32[4,1,98304]{2,1,0:T(1,128)S(1)}, u32[]{:S(2)}, u32[]{:S(2)}) async-start(f32[4,1,98304]{2,1,0:T(1,128)} %reshape.176), calls=%async_computation | async-start | bytes 3145728 | tf_op jit(solution)/shard_map/all_to_all | solution.py:149
  31.8 1.8 copy.65
  33.7 13.9 %all-to-all-done = f32[4,1,98304]{2,1,0:T(1,128)S(1)} async-done(((f32[4,1,98304]{2,1,0:T(1,128)}), f32[4,1,98304]{2,1,0:T(1,128)S(1)}, u32[]{:S(2)}, u32[]{:S(2)}) %all-to-all-start) | async-done | bytes 1572896 | tf_op jit(solution)/shard_map/all_to_all | solution.py:149
  47.6 1.2 copy-done.1
  49.3 6.2 %reduce.4 = f32[4,98304]{1,0:T(4,128)S(1)} reduce(f32[4,1,98304]{2,1,0:T(1,128)} %copy-done.1, f32[]{:T(128)} %broadcast.2764), dimensions={1}, to_apply=%all_to_all.25.reduce_sub_computation | reduce | bytes 3145732 | tf_op jit(solution)/shard_map/all_to_all | solution.py:149
  55.5 8.9 %reshape.177 = f32[1024,3,8,16]{3,2,1,0:T(8,128)} reshape(f32[4,98304]{1,0:T(4,128)S(1)} %reduce.4) | data formatting | bytes 3145728
  64.4 7.8 %copy.69 = f32[3,8,16,4,256]{4,3,2,1,0:T(4,128)S(1)} copy(f32[3,8,16,4,256]{2,1,0,4,3:T(8,128)} %bitcast.231) | data formatting | bytes 3145728 | tf_op jit(solution)/shard_map/all_to_all | solution.py:149
  75.5 4.3 %all-to-all-start.1 = ((f32[2,32,16,256]{3,2,0,1:T(8,128)}), f32[2,32,16,256]{3,2,0,1:T(8,128)}, u32[]{:S(2)}, u32[]{:S(2)}) async-start(f32[2,32,16,256]{3,2,0,1:T(8,128)} %copy.59), calls=%async_computation.1 | async-start | bytes 2097152 | tf_op jit(solution)/shard_map/all_to_all | solution.py:151
  80.8 2.5 %multiply_bitcast_fusion = f32[16,256,128]{2,0,1:T(8,128)} fusion(f32[256,16,128]{2,1,0:T(8,128)S(1)} %gather_fusion, f32[256]{0:T(256)S(1)} %convert_element_type.43, pred[256]{0:T(512)(128)(4,1)S(1)} %compare_and_fusion), kind=kLoop, calls=%fused_computation.5 | loop fusion | flops 1048576 | bytes 4195584 | tf_op jit(solution)/shard_map/mul | solution.py:110
  83.3 8.4 %all-to-all-done.1 = f32[2,32,16,256]{3,2,0,1:T(8,128)} async-done(((f32[2,32,16,256]{3,2,0,1:T(8,128)}), f32[2,32,16,256]{3,2,0,1:T(8,128)}, u32[]{:S(2)}, u32[]{:S(2)}) %all-to-all-start.1) | async-done | bytes 1048608 | tf_op jit(solution)/shard_map/all_to_all | solution.py:151
  91.8 13.5 %all-to-all-start.2 = ((f32[16,256,128]{2,0,1:T(8,128)}), f32[16,256,128]{2,0,1:T(8,128)}, u32[]{:S(2)}, u32[]{:S(2)}) async-start(f32[16,256,128]{2,0,1:T(8,128)} %multiply_bitcast_fusion), calls=%async_computation.2 | async-start | bytes 4194304 | tf_op jit(solution)/shard_map/all_to_all | solution.py:111
  110.2 1.9 copy.61
  112.6 1.7 fusion.137
  114.3 40.1 %all-to-all-done.2 = f32[16,256,128]{2,0,1:T(8,128)} async-done(((f32[16,256,128]{2,0,1:T(8,128)}), f32[16,256,128]{2,0,1:T(8,128)}, u32[]{:S(2)}, u32[]{:S(2)}) %all-to-all-start.2) | async-done | bytes 2097184 | tf_op jit(solution)/shard_map/all_to_all | solution.py:111
  154.4 3.4 %fusion.4 = f32[16,128,128]{2,1,0:T(8,128)S(1)} fusion(f32[256,128,1]{0,1,2:T(8,128)S(1)} %convolution_bitcast_fusion, f32[16,256,128]{2,0,1:T(8,128)} %all-to-all-done.2), kind=kOutput, calls=%fused_computation.12 | convolution fusion | flops 805306368 | bytes 3276800 | tf_op jit(solution)/shard_map/lic,ib->lbc/dot_general | solution.py:129
  158.0 1.4 add.2442
  159.6 2.0 collective-permute-start.1
  161.6 2.4 %collective-permute-start = (f32[34,1,1024]{2,1,0:T(1,128)S(1)}, f32[34,1,1024]{2,1,0:T(1,128)S(1)}, u32[]{:S(2)}, u32[]{:S(2)}) collective-permute-start(f32[34,1,1024]{2,1,0:T(1,128)S(1)} %get-tuple-element.83), channel_id=1, source_target_pairs={{16,0},{32,16},{48,32},{64,48},{80,64},{96,80},{112,96},{128,112},... | collective-permute-start | bytes 417800 | tf_op jit(solution)/shard_map/ppermute | solution.py:23
  164.4 3.6 %collective-permute-done = f32[34,1,1024]{2,1,0:T(1,128)S(1)} collective-permute-done((f32[34,1,1024]{2,1,0:T(1,128)S(1)}, f32[34,1,1024]{2,1,0:T(1,128)S(1)}, u32[]{:S(2)}, u32[]{:S(2)}) %collective-permute-start) | collective-permute-done | bytes 139296 | tf_op jit(solution)/shard_map/ppermute | solution.py:23
  168.7 1.7 fusion.135
  170.5 2.1 collective-permute-start.3
  172.6 2.6 %collective-permute-start.2 = (f32[17,1,1024]{2,1,0:T(1,128)S(1)}, f32[17,1,1024]{2,1,0:T(1,128)S(1)}, u32[]{:S(2)}, u32[]{:S(2)}) collective-permute-start(f32[17,1,1024]{2,1,0:T(1,128)S(1)} %get-tuple-element.87), channel_id=1, source_target_pairs={{16,0},{32,16},{48,32},{64,48},{80,64},{96,80},{112,96},{128,112},... | collective-permute-start | bytes 208904 | tf_op jit(solution)/shard_map/ppermute | solution.py:23
  175.2 1.7 fusion.35
  177.0 2.1 %reduce_sum.39 = f32[8,16,1024]{2,1,0:T(8,128)} reduce(f32[2,8,16,1024]{3,2,1,0:T(8,128)} %bitcast.265, f32[]{:T(128)} %constant.48.clone.1), dimensions={0}, to_apply=%region_7.8 | reduce | flops 131072 | bytes 1572868 | tf_op jit(solution)/shard_map/reduce_sum | solution.py:161
  181.4 3.2 %collective-permute-start.5 = (f32[17,1,1024]{2,1,0:T(1,128)S(1)}, f32[17,1,1024]{2,1,0:T(1,128)S(1)}, u32[]{:S(2)}, u32[]{:S(2)}) collective-permute-start(f32[17,1,1024]{2,1,0:T(1,128)S(1)} %get-tuple-element.86), channel_id=1, source_target_pairs={{0,16},{16,32},{32,48},{48,64},{64,80},{80,96},{96,112},{112,128},... | collective-permute-start | bytes 208904 | tf_op jit(solution)/shard_map/ppermute | solution.py:21
  185.0 1.9 collective-permute-start.4
  187.2 3.4 %collective-permute-done.4 = f32[17,1,1024]{2,1,0:T(1,128)S(1)} collective-permute-done((f32[17,1,1024]{2,1,0:T(1,128)S(1)}, f32[17,1,1024]{2,1,0:T(1,128)S(1)}, u32[]{:S(2)}, u32[]{:S(2)}) %collective-permute-start.4) | collective-permute-done | bytes 69664 | tf_op jit(solution)/shard_map/ppermute | solution.py:23
  190.6 1.6 fusion.27
  192.2 9.9 %reduce-scatter.2.cloned.1.call-done = f32[8,16,256]{2,1,0:T(8,128)} async-done(((f32[8,16,1024]{2,1,0:T(8,128)}), f32[8,16,256]{2,1,0:T(8,128)}) %reduce-scatter.2.cloned.1.call-update) | async-done | bytes 131088 | tf_op jit(solution)/shard_map/reduce_scatter | solution.py:160
  (134 shorter events, 17.3 us)
Async XLA Ops:
  23.9 5.0 %copy-start.2 = (f32[2,8,16,1024]{3,2,1,0:T(8,128)S(1)}, f32[2,8,16,1024]{3,2,1,0:T(8,128)}, u32[]{:S(2)}) copy-start(f32[2,8,16,1024]{3,2,1,0:T(8,128)} %param.11) | copy-start | bytes 3145732
  23.9 23.8 %all-to-all-start = ((f32[4,1,98304]{2,1,0:T(1,128)}), f32[4,1,98304]{2,1,0:T(1,128)S(1)}, u32[]{:S(2)}, u32[]{:S(2)}) async-start(f32[4,1,98304]{2,1,0:T(1,128)} %reshape.176), calls=%async_computation | async-start | bytes 3145728 | tf_op jit(solution)/shard_map/all_to_all | solution.py:149
  28.8 1.2 copy-start.10
  28.8 1.2 copy-start.12
  28.8 2.2 %copy-start.11 = (s32[16,256]{1,0:T(8,128)S(1)}, s32[16,256]{1,0:T(8,128)}, u32[]{:S(2)}) copy-start(s32[16,256]{1,0:T(8,128)} %param.19) | copy-start | bytes 49156
  47.6 1.2 copy-start.1
  75.5 16.3 %all-to-all-start.1 = ((f32[2,32,16,256]{3,2,0,1:T(8,128)}), f32[2,32,16,256]{3,2,0,1:T(8,128)}, u32[]{:S(2)}, u32[]{:S(2)}) async-start(f32[2,32,16,256]{3,2,0,1:T(8,128)} %copy.59), calls=%async_computation.1 | async-start | bytes 2097152 | tf_op jit(solution)/shard_map/all_to_all | solution.py:151
  83.3 24.8 %copy-start.8 = (f32[16,1024]{1,0:T(8,128)S(1)}, f32[16,1024]{1,0:T(8,128)}, u32[]{:S(2)}) copy-start(f32[16,1024]{1,0:T(8,128)} %param.16) | copy-start | bytes 196612
  83.3 24.9 %copy-start.9 = (f32[16,1024]{1,0:T(8,128)S(1)}, f32[16,1024]{1,0:T(8,128)}, u32[]{:S(2)}) copy-start(f32[16,1024]{1,0:T(8,128)} %param.14) | copy-start | bytes 196612
  91.8 62.6 %all-to-all-start.2 = ((f32[16,256,128]{2,0,1:T(8,128)}), f32[16,256,128]{2,0,1:T(8,128)}, u32[]{:S(2)}, u32[]{:S(2)}) async-start(f32[16,256,128]{2,0,1:T(8,128)} %multiply_bitcast_fusion), calls=%async_computation.2 | async-start | bytes 4194304 | tf_op jit(solution)/shard_map/all_to_all | solution.py:111
  105.3 96.8 %reduce-scatter.2.cloned.1.call-start = ((), (), s32[]{:S(2)}) async-start(), calls=%async_computation.4 | async-start | bytes 655360 | tf_op jit(solution)/shard_map/reduce_scatter | solution.py:160
  157.9 1.4 copy-start
  157.9 1.4 copy-start.7
  159.6 4.7 %collective-permute-start.1 = (f32[34,1,1024]{2,1,0:T(1,128)S(1)}, f32[34,1,1024]{2,1,0:T(1,128)S(1)}, u32[]{:S(2)}, u32[]{:S(2)}) collective-permute-start(f32[34,1,1024]{2,1,0:T(1,128)S(1)} %get-tuple-element.84), channel_id=1, source_target_pairs={{0,16},{16,32},{32,48},{48,64},{64,80},{80,96},{96,112},{112,128},... | collective-permute-start | bytes 417800 | tf_op jit(solution)/shard_map/ppermute | solution.py:21
  161.6 6.4 %collective-permute-start = (f32[34,1,1024]{2,1,0:T(1,128)S(1)}, f32[34,1,1024]{2,1,0:T(1,128)S(1)}, u32[]{:S(2)}, u32[]{:S(2)}) collective-permute-start(f32[34,1,1024]{2,1,0:T(1,128)S(1)} %get-tuple-element.83), channel_id=1, source_target_pairs={{16,0},{32,16},{48,32},{64,48},{80,64},{96,80},{112,96},{128,112},... | collective-permute-start | bytes 417800 | tf_op jit(solution)/shard_map/ppermute | solution.py:23
  168.7 6.5 %copy-start.6 = (f32[16,16,1023]{2,1,0:T(8,128)S(1)}, f32[16,16,1023]{2,1,0:T(8,128)}, u32[]{:S(2)}) copy-start(f32[16,16,1023]{2,1,0:T(8,128)} %get-tuple-element.96) | copy-start | bytes 3142660
  170.4 4.8 %copy-start.5 = (f32[16,16,1023]{2,1,0:T(8,128)S(1)}, f32[16,16,1023]{2,1,0:T(8,128)}, u32[]{:S(2)}) copy-start(f32[16,16,1023]{2,1,0:T(8,128)} %get-tuple-element.95) | copy-start | bytes 3142660
  170.5 8.6 %collective-permute-start.3 = (f32[17,1,1024]{2,1,0:T(1,128)S(1)}, f32[17,1,1024]{2,1,0:T(1,128)S(1)}, u32[]{:S(2)}, u32[]{:S(2)}) collective-permute-start(f32[17,1,1024]{2,1,0:T(1,128)S(1)} %get-tuple-element.88), channel_id=1, source_target_pairs={{0,16},{16,32},{32,48},{48,64},{64,80},{80,96},{96,112},{112,128},... | collective-permute-start | bytes 208904 | tf_op jit(solution)/shard_map/ppermute | solution.py:21
  172.6 6.8 %collective-permute-start.2 = (f32[17,1,1024]{2,1,0:T(1,128)S(1)}, f32[17,1,1024]{2,1,0:T(1,128)S(1)}, u32[]{:S(2)}, u32[]{:S(2)}) collective-permute-start(f32[17,1,1024]{2,1,0:T(1,128)S(1)} %get-tuple-element.87), channel_id=1, source_target_pairs={{16,0},{32,16},{48,32},{64,48},{80,64},{96,80},{112,96},{128,112},... | collective-permute-start | bytes 208904 | tf_op jit(solution)/shard_map/ppermute | solution.py:23
  179.1 1.2 copy-start.3
  179.1 1.5 copy-start.4
  181.4 5.5 %collective-permute-start.5 = (f32[17,1,1024]{2,1,0:T(1,128)S(1)}, f32[17,1,1024]{2,1,0:T(1,128)S(1)}, u32[]{:S(2)}, u32[]{:S(2)}) collective-permute-start(f32[17,1,1024]{2,1,0:T(1,128)S(1)} %get-tuple-element.86), channel_id=1, source_target_pairs={{0,16},{16,32},{32,48},{48,64},{64,80},{80,96},{96,112},{112,128},... | collective-permute-start | bytes 208904 | tf_op jit(solution)/shard_map/ppermute | solution.py:21
  185.0 5.6 %collective-permute-start.4 = (f32[17,1,1024]{2,1,0:T(1,128)S(1)}, f32[17,1,1024]{2,1,0:T(1,128)S(1)}, u32[]{:S(2)}, u32[]{:S(2)}) collective-permute-start(f32[17,1,1024]{2,1,0:T(1,128)S(1)} %get-tuple-element.85), channel_id=1, source_target_pairs={{16,0},{32,16},{48,32},{64,48},{80,64},{96,80},{112,96},{128,112},... | collective-permute-start | bytes 208904 | tf_op jit(solution)/shard_map/ppermute | solution.py:23
Sparse Core Ops, SparseCore 0:
  179.3 22.8 reduce-scatter.1
where the time goes:
time: 211 us; the launch traced here: 209 us
  waiting for transfers between devices  79.3 us (38%)
  local copies, waits for them, and re-layouts  49.5 us (23%)
  starting transfers between devices  36.9 us (17%)
  other arithmetic  24.7 us (12%)
  between operations  14.8 us (7%)
  matrix products  3.79 us (2%)
    all_to_all x1, waiting for transfers between devices, deliver(): lax.all_to_all(packed, 'tile', split_axis=1, concat_axis=1, tiled=True)  40.1 us
    unnamed x43, local copies, waits for them, and re-layouts  19.7 us
    all_to_all x1, waiting for transfers between devices, shards(): lax.all_to_all(stacked, 'lev', split_axis=3, concat_axis=1, tiled=True)  13.9 us
    all_to_all x1, starting transfers between devices, deliver(): lax.all_to_all(packed, 'tile', split_axis=1, concat_axis=1, tiled=True)  13.5 us
    reduce_scatter x1, waiting for transfers between devices, shards(): lax.psum_scatter(jnp.sum(parent_adjoint, axis=0), 'tag', scatter_dimensio...  9.95 us
    all_to_all x1, waiting for transfers between devices, shards(): lax.all_to_all(column_result, 'lev', split_axis=1, concat_axis=3, tiled=T...  8.45 us
    all_to_all x2, local copies, waits for them, and re-layouts, shards(): lax.all_to_all(stacked, 'lev', split_axis=3, concat_axis=1, tiled=True)  8.35 us
    ppermute x3, starting transfers between devices, extended(): lax.ppermute(tail, axis, [(i, (i + 1) % count) for i in range(ends)])  7.18 us
  transfers between devices with their start and end apart: 10, of which 6 were waited for; matrix products, arithmetic and copies ran while one was open for 12% of the time, Pallas kernels for 0%

commit v1 on v0

v1 whole, which is shorter than its diff:
```python
import functools

import jax
import jax.numpy as jnp
from jax import lax
from jax.experimental import pallas as pl
from jax.experimental.pallas import tpu as pltpu
from jax.sharding import PartitionSpec as P

MESH = pl.DeviceIdType.MESH
F32 = jnp.float32
BF16 = jnp.bfloat16
TILES = 16
CHIPS = 8
SLOTS = 16
LINES = 16
LEVELS = 8
ROWS = 16
COLS = 1024
LANES = 128
NBLK = 128
ENTRIES = 256
NSUB = 3
FULL = (112, 80, 48, 16)
USUAL = (64, 48, 40, 16)


def iota(shape, dim):
    return lax.broadcasted_iota(jnp.int32, shape, dim)


def chip_gap(to_tile, from_tile):
    return ((to_tile >> 1) - (from_tile >> 1)) & (CHIPS - 1)


def way_counts(gap, count):
    half = jnp.floor(count * 0.5)
    up = jnp.where((gap >= 1) & (gap <= 3), count, jnp.where(gap == 4, count - half, 0.0))
    down = jnp.where(gap >= 5, count, jnp.where(gap == 4, half, 0.0))
    return up, down


def way_keys(gap, tile):
    side = tile & 1
    return (4 - gap) * 2 + side, (gap - 4) * 2 + side


def counts_column(count_ref):
    row = iota((TILES, ENTRIES), 0)
    total = jnp.zeros((TILES, ENTRIES), jnp.int32)
    for tile in range(TILES):
        total = jnp.where(row == tile, count_ref[tile], total)
    return total


def plan_kernel(tile_ref, count_ref, flag_ref):
    live = iota((TILES, ENTRIES), 1) < counts_column(count_ref)
    listed = jnp.where(live, tile_ref[...], -1)
    nest = iota((TILES, 1), 0)

    def one(source, excess):
        count = jnp.sum(jnp.where(listed == source, 1.0, 0.0), axis=1, keepdims=True)
        gap = chip_gap(nest, source)
        up, down = way_counts(gap, count)
        for hop in range(1, 4):
            for load in (jnp.where(gap >= hop, up, 0.0), jnp.where(8 - gap >= hop, down, 0.0)):
                total = jnp.sum(load, axis=0, keepdims=True)
                excess = jnp.maximum(excess, total - USUAL[hop - 1])
        return excess

    excess = lax.fori_loop(0, TILES, one, jnp.zeros((1, 1), F32))
    flag_ref[0] = (jnp.max(excess) > 0.5).astype(jnp.int32)


def split(value):
    high = value.astype(BF16)
    low = (value - high.astype(F32)).astype(BF16)
    return high, low


def routed(matrix, value):
    high, low = split(value)
    return jnp.dot(matrix, high, preferred_element_type=F32) + jnp.dot(
        matrix, low, preferred_element_type=F32
    )


def onehot_product(left, right):
    return lax.dot_general(left, right, (((1,), (1,)), ((), ())), preferred_element_type=F32)


def blocks_of(ref, line):
    return jnp.concatenate(
        [ref[line, :, LANES * c : LANES * (c + 1)] for c in range(COLS // LANES)], axis=0
    )


def relax(x, top, bottom, coef):
    row = iota((ROWS, COLS), 0)
    above = jnp.where(row == 0, top, pltpu.roll(x, 1, 0))
    below = jnp.where(row == ROWS - 1, bottom, pltpu.roll(x, ROWS - 1, 0))
    west = pltpu.roll(x, 1, 1)
    east = pltpu.roll(x, COLS - 1, 1)
    return coef[0] * x + coef[1] * below + coef[2] * above + coef[3] * east + coef[4] * west


def coefficients(eastward, northward, north_above):
    col = iota(eastward.shape, 1)
    west = jnp.where(col == 0, 0.0, pltpu.roll(eastward, 1, 1))
    east = jnp.where(col == COLS - 1, 0.0, eastward)
    center = 1.0 - northward - north_above - eastward - west
    return center, northward, north_above, east, west


def relax_row(x, above, below, eastward, northward, north_above):
    wide = (LINES, COLS)
    center, north, north_up, east, west = coefficients(
        jnp.broadcast_to(eastward, (8, COLS)),
        jnp.broadcast_to(northward, (8, COLS)),
        jnp.broadcast_to(north_above, (8, COLS)),
    )
    center, north, north_up, east, west = (
        jnp.broadcast_to(v[:1], wide) for v in (center, north, north_up, east, west)
    )
    return (
        center * x
        + north * below
        + north_up * above
        + east * pltpu.roll(x, COLS - 1, 1)
        + west * pltpu.roll(x, 1, 1)
    )


def step_kernel(
    cap,
    parent,
    nest,
    mixing,
    parent_e,
    parent_n,
    nest_e,
    nest_n,
    strip_tile,
    strip_block,
    strip_target,
    strip_count,
    parent_out,
    nest_out,
    bulk_out,
    edges,
    pack_top,
    pack_bottom,
    coef_top,
    coef_bottom,
    slot_of,
    block_of,
    outgoing,
    near_out,
    near_in,
    got1,
    got2,
    got3,
    got4,
    route1,
    route2,
    route3,
    route4,
    route_near,
    route_own,
    solved,
    weight,
    message,
    from_outer,
    from_center,
    from_inner,
    rim_out,
    rim_in,
    parent_coef,
    nest_coef,
    tag_sum,
    tag_in,
    start,
    halo_out,
    halo_in,
    halos,
    send_sem,
    recv_sem,
):
    got = (None, got1, got2, got3, got4)
    route = (None, route1, route2, route3, route4)
    first = cap[0]
    tile = lax.axis_index("tile")
    lev = lax.axis_index("lev")
    tag = lax.axis_index("tag")
    sibling = tile + 1 - 2 * (tile % 2)
    ring = ((tile + 2) % TILES, (tile + TILES - 2) % TILES)
    tile_up = (tile + 1) % TILES
    tile_down = (tile + TILES - 1) % TILES
    mate = lev + 1 - 2 * (lev % 2)
    across = 3 - lev
    outer = lev % 3 == 0
    inner = lev % 3 != 0
    down = lev // 2

    barrier = pltpu.get_barrier_semaphore()
    peers = [{"tile": t} for t in (tile_up, tile_down) + ring]
    peers += [{"lev": (lev + d) % 4} for d in (1, 2, 3)]
    peers += [{"tag": (tag + d) % 4} for d in (1, 2, 3)]
    for peer in peers:
        pl.semaphore_signal(barrier, inc=1, device_id=peer, device_id_type=MESH)

    used = [0]
    pending = []

    def remote(src, dst, device, guard=None):
        at = used[0]
        used[0] += 1
        copy = pltpu.make_async_remote_copy(
            src_ref=src,
            dst_ref=dst,
            send_sem=send_sem.at[at],
            recv_sem=recv_sem.at[at],
            device_id=device,
            device_id_type=MESH,
        )
        pending.append((copy, guard))
        return copy

    pack_bottom[0:3] = nest_e[ROWS - 3 : ROWS]
    pack_bottom[3:6] = nest_n[ROWS - 3 : ROWS]
    pack_bottom[6:7] = parent_n[ROWS - 1 : ROWS]
    pack_bottom[7:8] = parent_n[ROWS - 1 : ROWS]
    pack_top[0:3] = nest_e[0:3]
    pack_top[3:6] = nest_n[0:3]
    pack_top[6:8] = parent_n[0:2]
    edges[0:LEVELS] = mixing[...]

    has_above = tile > 0
    has_below = tile < TILES - 1

    row = iota((TILES, ENTRIES), 0)
    entry = iota((TILES, ENTRIES), 1)
    live = entry < counts_column(strip_count)
    listed = jnp.where(live, strip_tile[...], -1)
    mine = jnp.where(listed == tile, 1.0, 0.0)
    upto = jnp.where(
        iota((ENTRIES, ENTRIES), 0) <= iota((ENTRIES, ENTRIES), 1), 1.0, 0.0
    ).astype(BF16)
    rank = jnp.dot(mine.astype(BF16), upto, preferred_element_type=F32) - 1.0
    count = jnp.broadcast_to(jnp.sum(mine, axis=1, keepdims=True), (TILES, ENTRIES))
    gap = chip_gap(row, tile)
    up_count, down_count = way_counts(gap, count)
    up_key, down_key = way_keys(gap, row)
    up_at = jnp.zeros((TILES, ENTRIES), F32)
    down_at = jnp.zeros((TILES, ENTRIES), F32)
    for other in range(TILES):
        up_at += jnp.where(up_key[other : other + 1] < up_key, up_count[other : other + 1], 0.0)
        down_at += jnp.where(
            down_key[other : other + 1] < down_key, down_count[other : other + 1], 0.0
        )
    half = jnp.floor(rank * 0.5)
    odd = rank - 2.0 * half
    goes_up = ((gap >= 1) & (gap <= 3)) | ((gap == 4) & (odd < 0.5))
    goes_down = (gap >= 5) | ((gap == 4) & (odd > 0.5))
    in_row = jnp.where(gap == 4, half, rank)
    slot = jnp.where(
        goes_up,
        up_at + in_row,
        jnp.where(
            goes_down,
            first + down_at + in_row,
            jnp.where((gap == 0) & (row != tile), 2 * first + rank, -1.0),
        ),
    )
    slot_of[...] = jnp.where(mine > 0.5, slot, -1.0)
    blocks = strip_block[...]
    block_of[...] = ((blocks & 7) * ROWS + (blocks >> 3) + 1).astype(F32)

    def gather_matrix(begin, size):
        wanted = (iota((size, ENTRIES), 0) + begin).astype(F32)

        def one(nest_tile, total):
            at = pl.ds(nest_tile, 1)
            return total + jnp.where(slot_of[at, :] == wanted, block_of[at, :], 0.0)

        total = lax.fori_loop(0, TILES, one, jnp.zeros((size, ENTRIES), F32))
        index = jnp.sum(total, axis=1, keepdims=True) - 1.0
        return jnp.where(index == iota((size, NBLK), 1).astype(F32), 1.0, 0.0).astype(BF16)

    gather = jnp.concatenate(
        [gather_matrix(0, first), gather_matrix(first, first), gather_matrix(2 * first, SLOTS)],
        axis=0,
    )

    def pack(pair, _):
        cells = jnp.concatenate([blocks_of(parent, 2 * pair), blocks_of(parent, 2 * pair + 1)], axis=1)
        taken = routed(gather, cells)
        for side in range(2):
            lanes = slice(LANES * side, LANES * (side + 1))
            outgoing[0, 2 * pair + side] = taken[:first, lanes]
            outgoing[1, 2 * pair + side] = taken[first : 2 * first, lanes]
            near_out[2 * pair + side] = taken[2 * first :, lanes]
        return 0

    lax.fori_loop(0, LINES // 2, pack, 0)

    pl.semaphore_wait(barrier, len(peers))

    edge_copy = remote(edges.at[0], edges.at[LEVELS], {"lev": (lev + 3) % 4}, lev > 0)
    pl.when(lev > 0)(edge_copy.start)
    pack_down_copy = remote(pack_bottom, coef_top, {"tile": tile_up}, has_below)
    pl.when(has_below)(pack_down_copy.start)
    pack_up_copy = remote(pack_top, coef_bottom, {"tile": tile_down}, has_above)
    pl.when(has_above)(pack_up_copy.start)

    near_copy = remote(near_out, near_in, {"tile": sibling})
    near_copy.start()
    cuts = (0, cap[3], cap[2], cap[1], cap[0])
    hop_copy = {}
    for hop in range(1, 5):
        for piece in range(5 - hop):
            for way in range(2):
                part = pl.ds(cuts[piece], cuts[piece + 1] - cuts[piece])
                src = outgoing if hop == 1 else got[hop - 1]
                hop_copy[hop, piece, way] = remote(
                    src.at[way, :, part, :], got[hop].at[way, :, part, :], {"tile": ring[way]}
                )
    side_copy = {}
    for hop in range(1, 5):
        for way in range(2):
            side_copy[hop, way] = remote(got[hop].at[way], got[hop].at[2 + way], {"tile": sibling})
    for piece in range(4):
        for way in range(2):
            hop_copy[1, piece, way].start()

    def relay(hop, piece):
        for way in range(2):
            hop_copy[hop - 1, piece, way].wait_recv()
            hop_copy[hop, piece, way].start()

    def share(hop):
        for way in range(2):
            hop_copy[hop, 4 - hop, way].wait_recv()
            side_copy[hop, way].start()

    pl.when(lev < 3)(edge_copy.wait_recv)

    @pl.when(lev == 3)
    def _():
        edges[LEVELS] = jnp.zeros((ROWS, COLS), F32)

    def level(step):
        return step + down * (LEVELS - 1 - 2 * step)

    def field(which, at, rows):
        return parent[which * LEVELS + at, rows, :]

    def sweep(rows, pivot, value0, value1):
        for step in range(LEVELS):
            at = level(step)
            edge = edges[at + 1 - down, rows, :]
            inverse = 1.0 / (pivot + edge)
            ratio = edge * inverse
            carry0 = value0 * inverse
            carry1 = value1 * inverse
            solved[at, rows, :] = carry0
            solved[LEVELS + at, rows, :] = carry1
            weight[at, rows, :] = ratio
            if step < LEVELS - 1:
                follow = level(step + 1)
                pivot = 1.0 + ratio * pivot
                value0 = field(0, follow, rows) + edge * carry0
                value1 = field(1, follow, rows) + edge * carry1
        message[0, rows, :] = pivot
        message[1, rows, :] = value0
        message[2, rows, :] = value1

    def back(rows, value0, value1, last):
        for step in range(last, -1, -1):
            at = level(step)
            ratio = weight[at, rows, :]
            value0 = solved[at, rows, :] + ratio * value0
            value1 = solved[LEVELS + at, rows, :] + ratio * value1
            solved[at, rows, :] = value0
            solved[LEVELS + at, rows, :] = value1

    halves = [pl.ds(0, 8), pl.ds(8, 8)]
    near_level = level(0)
    outer_copy = [
        remote(message.at[:, rows, :], from_outer.at[:, rows, :], {"lev": mate}, outer)
        for rows in halves
    ]
    center_copy = [
        remote(message.at[:, rows, :], from_center.at[:, rows, :], {"lev": across}, inner)
        for rows in halves
    ]
    inner_copy = [
        [
            remote(
                solved.at[which * LEVELS + near_level, rows, :],
                from_inner.at[which, rows, :],
                {"lev": mate},
                inner,
            )
            for which in range(2)
        ]
        for rows in halves
    ]

    @pl.when(outer)
    def _():
        for part, rows in enumerate(halves):
            at = level(0)
            sweep(rows, 1.0 + edges[at + down, rows, :], field(0, at, rows), field(1, at, rows))
            outer_copy[part].start()

    own_tiles = strip_tile[pl.ds(tile, 1), :]
    own_live = iota((1, ENTRIES), 1) < strip_count[tile]
    own_tiles = jnp.where(own_live, own_tiles, -1)
    source_row = iota((TILES, ENTRIES), 0)
    from_source = jnp.where(own_tiles == source_row, 1.0, 0.0)
    own_rank = jnp.sum(
        from_source
        * (jnp.dot(from_source.astype(BF16), upto, preferred_element_type=F32) - 1.0),
        axis=0,
        keepdims=True,
    )
    nest_column = iota((TILES, 1), 0)

    def offsets(source, totals):
        up_total, down_total = totals
        count = jnp.sum(jnp.where(listed == source, 1.0, 0.0), axis=1, keepdims=True)
        gap = chip_gap(nest_column, source)
        up, down_ = way_counts(gap, count)
        up_key, down_key = way_keys(gap, nest_column)
        own_up, own_down = way_keys(chip_gap(tile, source), tile)
        up_here = jnp.sum(jnp.where(up_key < own_up, up, 0.0), axis=0, keepdims=True)
        down_here = jnp.sum(jnp.where(down_key < own_down, down_, 0.0), axis=0, keepdims=True)
        here = own_tiles == source
        return (
            up_total + jnp.where(here, up_here, 0.0),
            down_total + jnp.where(here, down_here, 0.0),
        )

    nothing = jnp.zeros((1, ENTRIES), F32)
    up_start, down_start = lax.fori_loop(0, TILES, offsets, (nothing, nothing))
    own_gap = jnp.where(own_tiles >= 0, chip_gap(tile, own_tiles), -1)
    own_half = jnp.floor(own_rank * 0.5)
    own_odd = own_rank - 2.0 * own_half
    comes_up = ((own_gap >= 1) & (own_gap <= 3)) | ((own_gap == 4) & (own_odd < 0.5))
    place = jnp.where(own_gap == 4, own_half, own_rank) + jnp.where(comes_up, up_start, down_start)
    hops = jnp.where(own_gap >= 1, jnp.where(comes_up, own_gap, CHIPS - own_gap), 0)
    group = jnp.where((own_tiles & 1) == (tile & 1), 0.0, 2.0) + jnp.where(comes_up, 0.0, 1.0)
    targets = strip_target[pl.ds(tile, 1), :]
    targets = jnp.where(own_tiles >= 0, (targets & 7) * ROWS + (targets >> 3), -1)
    lands = jnp.where(targets == iota((NBLK, ENTRIES), 0), 1.0, 0.0).astype(BF16)

    def picks(place, rows):
        return jnp.where(place == iota((rows, ENTRIES), 0).astype(F32), 1.0, 0.0).astype(BF16)

    for hop in range(1, 5):
        size = cap[hop - 1]
        at = jnp.where(hops == hop, group * size + place, -1.0)
        route[hop][...] = onehot_product(lands, picks(at, 4 * size)).astype(BF16)
    at = jnp.where((own_gap == 0) & (own_tiles != tile), own_rank, -1.0)
    route_near[...] = onehot_product(lands, picks(at, SLOTS)).astype(BF16)
    own_blocks = strip_block[pl.ds(tile, 1), :]
    own_blocks = jnp.where(own_tiles == tile, (own_blocks & 7) * ROWS + (own_blocks >> 3), -1)
    route_own[...] = onehot_product(lands, picks(own_blocks.astype(F32), NBLK)).astype(BF16)

    @pl.when(inner)
    def _():
        for part, rows in enumerate(halves):
            at = level(0)
            outer_copy[part].wait_recv()
            edge = edges[at + down, rows, :]
            pivot = from_outer[0, rows, :]
            ratio = edge / (pivot + edge)
            sweep(
                rows,
                1.0 + ratio * pivot,
                field(0, at, rows) + ratio * from_outer[1, rows, :],
                field(1, at, rows) + ratio * from_outer[2, rows, :],
            )
            center_copy[part].start()

    relay(2, 0)
    relay(2, 1)

    @pl.when(inner)
    def _():
        for part, rows in enumerate(halves):
            center_copy[part].wait_recv()
            at = level(LEVELS - 1)
            edge = edges[at + 1 - down, rows, :]
            pivot = from_center[0, rows, :]
            ratio = edge / (pivot + edge)
            inverse = 1.0 / (message[0, rows, :] + ratio * pivot)
            value0 = (message[1, rows, :] + ratio * from_center[1, rows, :]) * inverse
            value1 = (message[2, rows, :] + ratio * from_center[2, rows, :]) * inverse
            solved[at, rows, :] = value0
            solved[LEVELS + at, rows, :] = value1
            back(rows, value0, value1, LEVELS - 2)
            for copy in inner_copy[part]:
                copy.start()

    @pl.when(has_above)
    def _():
        pack_down_copy.wait_recv()

    @pl.when(has_below)
    def _():
        pack_up_copy.wait_recv()

    @pl.when(tile == 0)
    def _():
        coef_top[...] = jnp.zeros((8, COLS), F32)

    @pl.when(tile == TILES - 1)
    def _():
        coef_bottom[...] = jnp.zeros((8, COLS), F32)

    cell_row = iota((ROWS, COLS), 0)
    for target, e_ref, n_ref, above in (
        (parent_coef, parent_e, parent_n, coef_top[6:7]),
        (nest_coef, nest_e, nest_n, coef_top[5:6]),
    ):
        northward = n_ref[...]
        north_above = jnp.where(cell_row == 0, above, pltpu.roll(northward, 1, 0))
        for which, value in enumerate(coefficients(e_ref[...], northward, north_above)):
            target[which] = value

    relay(2, 2)

    @pl.when(outer)
    def _():
        for part, rows in enumerate(halves):
            for copy in inner_copy[part]:
                copy.wait_recv()
            back(rows, from_inner[0, rows, :], from_inner[1, rows, :], LEVELS - 1)

    for line in range(LINES):
        rim_out[0, line : line + 1] = solved[line, 0:1, :]
        rim_out[1, line : line + 1] = solved[line, ROWS - 1 : ROWS, :]
    rim_up = remote(rim_out.at[0], rim_in.at[1], {"tile": tile_down}, has_above)
    rim_down = remote(rim_out.at[1], rim_in.at[0], {"tile": tile_up}, has_below)
    pl.when(has_above)(rim_up.start)
    pl.when(has_below)(rim_down.start)

    share(1)

    near_copy.wait_recv()

    def add_blocks(line, taken):
        for c in range(COLS // LANES):
            start[line, :, LANES * c : LANES * (c + 1)] += taken[ROWS * c : ROWS * (c + 1)]

    def scatter_near(pair, _):
        cells = jnp.concatenate([blocks_of(parent, 2 * pair), blocks_of(parent, 2 * pair + 1)], axis=1)
        near = jnp.concatenate([near_in[2 * pair], near_in[2 * pair + 1]], axis=1)
        taken = routed(route_own[...], cells) + routed(route_near[...], near)
        for side in range(2):
            line = 2 * pair + side
            start[line] = nest[line]
            add_blocks(line, taken[:, LANES * side : LANES * (side + 1)])
        return 0

    lax.fori_loop(0, LINES // 2, scatter_near, 0)

    def scatter(hop):
        for way in range(2):
            side_copy[hop, way].wait_recv()

        def one(pair, _):
            cells = jnp.concatenate(
                [
                    jnp.concatenate([got[hop][g, 2 * pair + side] for g in range(4)], axis=0)
                    for side in range(2)
                ],
                axis=1,
            )
            taken = routed(route[hop][...], cells)
            for side in range(2):
                add_blocks(2 * pair + side, taken[:, LANES * side : LANES * (side + 1)])
            return 0

        lax.fori_loop(0, LINES // 2, one, 0)

    relay(3, 0)
    relay(3, 1)

    pl.when(has_above)(rim_down.wait_recv)
    pl.when(has_below)(rim_up.wait_recv)

    @pl.when(tile == 0)
    def _():
        rim_in[0] = jnp.zeros((LINES, COLS), F32)

    @pl.when(tile == TILES - 1)
    def _():
        rim_in[1] = jnp.zeros((LINES, COLS), F32)

    def parent_level(at, _):
        total = None
        for which in range(2):
            line = which * LEVELS + at
            result = relax(
                solved[line], rim_in[0, pl.ds(line, 1), :], rim_in[1, pl.ds(line, 1), :], parent_coef
            )
            parent_out[line] = result
            total = result if total is None else total + result
        tag_sum[at] = total
        return 0

    lax.fori_loop(0, LEVELS, parent_level, 0)

    quarter = COLS // 4

    def columns(which):
        return pl.ds(pl.multiple_of(which * quarter, quarter), quarter)

    tag_copy = []
    for d in (1, 2, 3):
        to = (tag + d) % 4
        copy = remote(tag_sum.at[:, :, columns(to)], tag_in.at[d - 1], {"tag": to})
        copy.start()
        tag_copy.append(copy)

    share(2)
    scatter(1)
    relay(4, 0)
    share(3)
    scatter(2)
    for copy in tag_copy:
        copy.wait_recv()
    bulk_out[...] = tag_sum[:, :, columns(tag)] + tag_in[0] + tag_in[1] + tag_in[2]
    share(4)
    scatter(3)
    scatter(4)

    for line in range(LINES):
        for r in range(NSUB):
            halo_out[0, r, line : line + 1] = start[line, r : r + 1, :]
            at = ROWS - NSUB + r
            halo_out[1, r, line : line + 1] = start[line, at : at + 1, :]
    halo_up = remote(halo_out.at[0], halo_in.at[1], {"tile": tile_down}, has_above)
    halo_down = remote(halo_out.at[1], halo_in.at[0], {"tile": tile_up}, has_below)
    pl.when(has_above)(halo_up.start)
    pl.when(has_below)(halo_down.start)
    pl.when(has_above)(halo_down.wait_recv)
    pl.when(has_below)(halo_up.wait_recv)

    @pl.when(tile == 0)
    def _():
        halo_in[0] = jnp.zeros((NSUB, LINES, COLS), F32)

    @pl.when(tile == TILES - 1)
    def _():
        halo_in[1] = jnp.zeros((NSUB, LINES, COLS), F32)

    in_grid = jnp.where(has_below, 1.0, 0.0)

    def e_top(r):
        return coef_top[r : r + 1]

    def n_top(r):
        return coef_top[3 + r : 4 + r]

    def e_bottom(r):
        return coef_bottom[r : r + 1]

    def n_bottom(r):
        return coef_bottom[3 + r : 4 + r]

    def own(ref, r):
        return ref[r : r + 1]

    second = relax_row(halo_in[0, 1], halo_in[0, 0], halo_in[0, 2], e_top(1), n_top(1), n_top(0))
    third = relax_row(halo_in[0, 2], halo_in[0, 1], halo_out[0, 0], e_top(2), n_top(2), n_top(1))
    edge_row = relax_row(
        halo_out[0, 0], halo_in[0, 2], halo_out[0, 1], own(nest_e, 0), own(nest_n, 0), n_top(2)
    )
    halos[0, 0] = halo_in[0, 2]
    halos[0, 1] = third
    halos[0, 2] = relax_row(third, second, edge_row, e_top(2), n_top(2), n_top(1))
    last = ROWS - 1
    second = relax_row(
        halo_in[1, 1], halo_in[1, 0], halo_in[1, 2], e_bottom(1), n_bottom(1), n_bottom(0)
    )
    third = in_grid * relax_row(
        halo_in[1, 0], halo_out[1, 2], halo_in[1, 1], e_bottom(0), n_bottom(0), own(nest_n, last)
    )
    edge_row = relax_row(
        halo_out[1, 2],
        halo_out[1, 1],
        halo_in[1, 0],
        own(nest_e, last),
        own(nest_n, last),
        own(nest_n, last - 1),
    )
    halos[1, 0] = halo_in[1, 0]
    halos[1, 1] = third
    halos[1, 2] = in_grid * relax_row(
        third, edge_row, second, e_bottom(0), n_bottom(0), own(nest_n, last)
    )

    def nest_line(line, _):
        value = start[line]
        for step in range(NSUB):
            value = relax(
                value, halos[0, step, pl.ds(line, 1), :], halos[1, step, pl.ds(line, 1), :], nest_coef
            )
        nest_out[line] = value
        return 0

    lax.fori_loop(0, LINES, nest_line, 0)

    for copy, guard in pending:
        if guard is None:
            copy.wait_send()
        else:
            pl.when(guard)(copy.wait_send)


VMEM = pl.BlockSpec(memory_space=pltpu.VMEM)
SMEM = pl.BlockSpec(memory_space=pltpu.SMEM)


def step_call(cap, collective, arrays):
    first = cap[0]
    grid = (LINES, ROWS, COLS)
    copies = 3 + 1 + 20 + 8 + 2 + 2 + 4 + 2 + 3 + 2
    shapes = [
        pltpu.VMEM((LEVELS + 1, ROWS, COLS), F32),
        pltpu.VMEM((8, COLS), F32),
        pltpu.VMEM((8, COLS), F32),
        pltpu.VMEM((8, COLS), F32),
        pltpu.VMEM((8, COLS), F32),
        pltpu.VMEM((TILES, ENTRIES), F32),
        pltpu.VMEM((TILES, ENTRIES), F32),
        pltpu.VMEM((2, LINES, first, LANES), F32),
        pltpu.VMEM((LINES, SLOTS, LANES), F32),
        pltpu.VMEM((LINES, SLOTS, LANES), F32),
    ]
    shapes += [pltpu.VMEM((4, LINES, size, LANES), F32) for size in cap]
    shapes += [pltpu.VMEM((NBLK, 4 * size), BF16) for size in cap]
    shapes += [
        pltpu.VMEM((NBLK, SLOTS), BF16),
        pltpu.VMEM((NBLK, NBLK), BF16),
        pltpu.VMEM(grid, F32),
        pltpu.VMEM((LEVELS, ROWS, COLS), F32),
        pltpu.VMEM((3, ROWS, COLS), F32),
        pltpu.VMEM((3, ROWS, COLS), F32),
        pltpu.VMEM((3, ROWS, COLS), F32),
        pltpu.VMEM((2, ROWS, COLS), F32),
        pltpu.VMEM((2, LINES, COLS), F32),
        pltpu.VMEM((2, LINES, COLS), F32),
        pltpu.VMEM((5, ROWS, COLS), F32),
        pltpu.VMEM((5, ROWS, COLS), F32),
        pltpu.VMEM((LEVELS, ROWS, COLS), F32),
        pltpu.VMEM((3, LEVELS, ROWS, COLS // 4), F32),
        pltpu.VMEM(grid, F32),
        pltpu.VMEM((2, NSUB, LINES, COLS), F32),
        pltpu.VMEM((2, NSUB, LINES, COLS), F32),
        pltpu.VMEM((2, NSUB, LINES, COLS), F32),
        pltpu.SemaphoreType.DMA((copies,)),
        pltpu.SemaphoreType.DMA((copies,)),
    ]
    return pl.pallas_call(
        functools.partial(step_kernel, cap),
        out_shape=[
            jax.ShapeDtypeStruct(grid, F32),
            jax.ShapeDtypeStruct(grid, F32),
            jax.ShapeDtypeStruct((LEVELS, ROWS, COLS // 4), F32),
        ],
        in_specs=[VMEM] * 10 + [SMEM],
        out_specs=[VMEM] * 3,
        scratch_shapes=shapes,
        compiler_params=pltpu.CompilerParams(
            collective_id=collective, has_side_effects=True, vmem_limit_bytes=56 * 1024 * 1024
        ),
    )(*arrays)


def shards(
    parent_field,
    nest_field,
    parent_mixing,
    parent_eastward,
    parent_northward,
    nest_eastward,
    nest_northward,
    strip_tile,
    strip_block,
    strip_target,
    strip_count,
):
    full_shape = parent_field.shape
    grid = (LINES, ROWS, COLS)
    arrays = (
        parent_field.reshape(grid),
        nest_field.reshape(grid),
        parent_mixing,
        parent_eastward,
        parent_northward,
        nest_eastward,
        nest_northward,
        strip_tile,
        strip_block,
        strip_target,
        strip_count,
    )
    flag = pl.pallas_call(
        plan_kernel,
        out_shape=jax.ShapeDtypeStruct((1,), jnp.int32),
        in_specs=[VMEM, SMEM],
        out_specs=SMEM,
    )(strip_tile, strip_count)
    parent_adjoint, nest_adjoint, bulk_adjoint = lax.cond(
        flag[0] > 0,
        lambda *a: step_call(FULL, 1, a),
        lambda *a: step_call(USUAL, 2, a),
        *arrays,
    )
    return parent_adjoint.reshape(full_shape), nest_adjoint.reshape(full_shape), bulk_adjoint


def solution(mesh):
    in_specs = (
        P("tag", "lev", "tile", None),
        P("tag", "lev", "tile", None),
        P("lev", "tile", None),
        P("tile", None),
        P("tile", None),
        P("tile", None),
        P("tile", None),
        P(),
        P(),
        P(),
        P(),
    )
    out_specs = (
        P("tag", "lev", "tile", None),
        P("tag", "lev", "tile", None),
        P("lev", "tile", "tag"),
    )
    return jax.shard_map(shards, mesh=mesh, in_specs=in_specs, out_specs=out_specs, check_vma=False)
```

time: 211 us -> 63.8 us (0.30)
  waiting for transfers between devices: 79.3 us -> 0 us
  Pallas kernels: 0 us -> 58.3 us
  local copies, waits for them, and re-layouts: 49.5 us -> 3.96 us
  starting transfers between devices: 36.9 us -> 0 us
  other arithmetic: 24.7 us -> 0 us
  between operations: 14.8 us -> 1.32 us
  matrix products: 3.79 us -> 0 us
    all_to_all x3 -> x0, waiting for transfers between devices: 62.4 us -> none  [the longest x1 40.1 us: deliver(): lax.all_to_all(packed, 'tile', split_axis=1, concat_axis=1, tiled=True)]
    pallas_call x0 -> x2, Pallas kernels: none -> 58.3 us  [the longest x1 55.3 us: step_call(): pl.pallas_call(functools.partial(step_kernel, cap), out_shape=[jax.ShapeD...]
    all_to_all x3 -> x0, starting transfers between devices: 22.8 us -> none  [the longest x1 13.5 us: deliver(): lax.all_to_all(packed, 'tile', split_axis=1, concat_axis=1, tiled=True)]
    unnamed x43 -> x7, local copies, waits for them, and re-layouts: 19.7 us -> 3.24 us
    ppermute x6 -> x0, starting transfers between devices: 14.1 us -> none  [the longest x3 7.18 us: extended(): lax.ppermute(tail, axis, [(i, (i + 1) % count) for i in range(ends)])]
    all_to_all x3 -> x0, local copies, waits for them, and re-layouts: 10.3 us -> none  [the longest x2 8.35 us: shards(): lax.all_to_all(stacked, 'lev', split_axis=3, concat_axis=1, tiled=True)]
    reduce_scatter x1 -> x0, waiting for transfers between devices: 9.95 us -> none  [shards(): lax.psum_scatter(jnp.sum(parent_adjoint, axis=0), 'tag', scatter_dimensio...]
    concatenate x3 -> x0, local copies, waits for them, and re-layouts: 7.08 us -> none  [the longest x1 6.92 us: shards(): stacked = jnp.concatenate([parent_field, parent_mixing[None]], axis=0)]
  transfers between devices with their start and end apart: 10 -> 0, of which waited for: 6 -> 0; matrix products, arithmetic and copies ran while one was open for 12% -> 0% of each run, Pallas kernels for 0% -> 0%
where the time goes in v1:
time: 63.8 us; the launch traced here: 63.6 us
  Pallas kernels  58.3 us (91%)
  local copies, waits for them, and re-layouts  3.96 us (6%)
  between operations  1.32 us (2%)
    pallas_call x1, Pallas kernels, step_call(): pl.pallas_call(functools.partial(step_kernel, cap), out_shape=[jax.ShapeD...  55.3 us
    unnamed x7, local copies, waits for them, and re-layouts  3.24 us
    pallas_call x1, Pallas kernels, shards(): pl.pallas_call(plan_kernel, out_shape=jax.ShapeDtypeStruct((1,), jnp.int3...  2.96 us

profile of v1, /device:TPU:1, one launch (start us, length us, event | category | flops | bytes accessed | tf_op | source)
XLA Modules:
  0.0 63.6 jit_solution(13149275824458975894)
XLA Ops:
  0.6 0.0 copy-start
  0.6 3.0 %shard_map.130 = s32[1]{0:T(128)} custom-call(s32[16,256]{1,0:T(8,128)} %tile_ref.1, s32[16]{0:T(128)} %count_ref.1), custom_call_target="tpu_custom_call" | custom-call | tf_op jit(solution)/shard_map/pallas_call | solution.py:813
  4.3 0.0 copy-start.3
  4.3 0.0 copy-done
  4.3 0.6 %copy-done.3 = s32[16]{0:T(128)S(1)} copy-done((s32[16]{0:T(128)S(1)}, s32[16]{0:T(128)}, u32[]{:S(2)}) %copy-start.3) | copy-done | bytes 88
  4.9 56.0 %conditional.1 = (f32[8,16,256]{2,1,0:T(8,128)S(1)}, f32[2,8,16,1024]{3,2,1,0:T(8,128)S(1)}, f32[2,8,16,1024]{3,2,1,0:T(8,128)S(1)}) conditional(s32[]{:T(128)} %bitcast.4, (f32[16,16,1024]{2,1,0:T(8,128)}, f32[16,16,1024]{2,1,0:T(8,128)}, f32[8,16,1024]{2,1,0:T(8,128)}, f32[16,1024]{1,0:T(8,128)}, f32[16,1024]{1,0:T(8,128)}, ...), branch_computations={%region_0.0_spmd, %region_1.0_spmd} | conditional | bytes 65588 | solution.py:819
  4.9 0.0 copy-start.1
  4.9 0.7 %copy-done.1 = s32[16,256]{1,0:T(8,128)S(1)} copy-done((s32[16,256]{1,0:T(8,128)S(1)}, s32[16,256]{1,0:T(8,128)}, u32[]{:S(2)}) %copy-start.1) | copy-done | bytes 16408 | tf_op jit(solution)/shard_map/cond
  5.6 55.3 %branch_0_fun.1 = (f32[16,16,1024]{2,1,0:T(8,128)S(1)}, f32[16,16,1024]{2,1,0:T(8,128)S(1)}, f32[8,16,256]{2,1,0:T(8,128)S(1)}) custom-call(f32[16,16,1024]{2,1,0:T(8,128)} %get-tuple-element.52.parent, f32[16,16,1024]{2,1,0:T(8,128)} %get-tuple-element.53.nest, f32[8,16,1024]{2,1,0:T(8,128)} %get-tuple-element.54.mixing, ...), custom_call_target="tpu_custom_call" | custom-call | tf_op jit(solution)/shard_map/cond/branch_0_fun/pallas_call | solution.py:769
  61.0 1.0 %copy.23 = f32[2,8,16,1024]{3,2,1,0:T(8,128)} copy(f32[2,8,16,1024]{3,2,1,0:T(8,128)S(1)} %get-tuple-element.98) | data formatting | bytes 2097152
  61.9 1.0 %copy.24 = f32[2,8,16,1024]{3,2,1,0:T(8,128)} copy(f32[2,8,16,1024]{3,2,1,0:T(8,128)S(1)} %get-tuple-element.99) | data formatting | bytes 2097152
  62.9 0.7 %copy.25 = f32[8,16,256]{2,1,0:T(8,128)} copy(f32[8,16,256]{2,1,0:T(8,128)S(1)} %get-tuple-element.100) | data formatting | bytes 262144
Async XLA Ops:
  0.6 3.6 %copy-start = (s32[16,256]{1,0:T(8,128)S(1)}, s32[16,256]{1,0:T(8,128)}, u32[]{:S(2)}) copy-start(s32[16,256]{1,0:T(8,128)} %tile_ref.1) | copy-start | bytes 49156
  4.3 0.7 %copy-start.3 = (s32[16]{0:T(128)S(1)}, s32[16]{0:T(128)}, u32[]{:S(2)}) copy-start(s32[16]{0:T(128)} %count_ref.1) | copy-start | bytes 196
  4.9 0.7 %copy-start.1 = (s32[16,256]{1,0:T(8,128)S(1)}, s32[16,256]{1,0:T(8,128)}, u32[]{:S(2)}) copy-start(s32[16,256]{1,0:T(8,128)} %get-tuple-element.60.strip_block) | copy-start | bytes 49156 | tf_op jit(solution)/shard_map/cond

commit v2 on v1

--- a/solution.py
+++ b/solution.py
@@ -23,6 +23,7 @@
 NSUB = 3
 FULL = (112, 80, 48, 16)
 USUAL = (64, 48, 40, 16)
+SMALL = (56, 40, 32, 16)
 
 
 def iota(shape, dim):
@@ -56,20 +57,22 @@
 def plan_kernel(tile_ref, count_ref, flag_ref):
     live = iota((TILES, ENTRIES), 1) < counts_column(count_ref)
     listed = jnp.where(live, tile_ref[...], -1)
-    nest = iota((TILES, 1), 0)
-
-    def one(source, excess):
-        count = jnp.sum(jnp.where(listed == source, 1.0, 0.0), axis=1, keepdims=True)
-        gap = chip_gap(nest, source)
-        up, down = way_counts(gap, count)
-        for hop in range(1, 4):
-            for load in (jnp.where(gap >= hop, up, 0.0), jnp.where(8 - gap >= hop, down, 0.0)):
-                total = jnp.sum(load, axis=0, keepdims=True)
-                excess = jnp.maximum(excess, total - USUAL[hop - 1])
-        return excess
-
-    excess = lax.fori_loop(0, TILES, one, jnp.zeros((1, 1), F32))
-    flag_ref[0] = (jnp.max(excess) > 0.5).astype(jnp.int32)
+    lane = iota((TILES, LANES), 1)
+    count = jnp.zeros((TILES, LANES), F32)
+    for source in range(TILES):
+        total = jnp.sum(jnp.where(listed == source, 1.0, 0.0), axis=1, keepdims=True)
+        count = jnp.where(lane == source, total, count)
+    gap = chip_gap(iota((TILES, LANES), 0), lane)
+    up, down = way_counts(gap, count)
+    small = jnp.zeros((1, LANES), F32)
+    usual = jnp.zeros((1, LANES), F32)
+    for hop in range(1, 4):
+        for load in (jnp.where(gap >= hop, up, 0.0), jnp.where(CHIPS - gap >= hop, down, 0.0)):
+            total = jnp.sum(load, axis=0, keepdims=True)
+            small = jnp.maximum(small, total - SMALL[hop - 1])
+            usual = jnp.maximum(usual, total - USUAL[hop - 1])
+    over = jnp.where(small > 0.5, 1.0, 0.0) + jnp.where(usual > 0.5, 1.0, 0.0)
+    flag_ref[0] = jnp.max(over).astype(jnp.int32)
 
 
 def split(value):
@@ -95,13 +98,28 @@
     )
 
 
-def relax(x, top, bottom, coef):
-    row = iota((ROWS, COLS), 0)
-    above = jnp.where(row == 0, top, pltpu.roll(x, 1, 0))
-    below = jnp.where(row == ROWS - 1, bottom, pltpu.roll(x, ROWS - 1, 0))
-    west = pltpu.roll(x, 1, 1)
-    east = pltpu.roll(x, COLS - 1, 1)
-    return coef[0] * x + coef[1] * below + coef[2] * above + coef[3] * east + coef[4] * west
+def relax(halves, top, bottom, coef):
+    row = iota((8, COLS), 0)
+    later = [pltpu.roll(x, 1, 0) for x in halves]
+    sooner = [pltpu.roll(x, 7, 0) for x in halves]
+    above = (jnp.where(row == 0, top, later[0]), jnp.where(row == 0, later[0], later[1]))
+    below = (jnp.where(row == 7, sooner[1], sooner[0]), jnp.where(row == 7, bottom, sooner[1]))
+    results = []
+    for part in range(2):
+        x = halves[part]
+        rows = slice(8 * part, 8 * part + 8)
+        results.append(
+            coef[0, rows] * x
+            + coef[1, rows] * below[part]
+            + coef[2, rows] * above[part]
+            + coef[3, rows] * pltpu.roll(x, COLS - 1, 1)
+            + coef[4, rows] * pltpu.roll(x, 1, 1)
+        )
+    return results
+
+
+def halves_of(ref, line):
+    return [ref[line, 0:8, :], ref[line, 8:16, :]]
 
 
 def coefficients(eastward, northward, north_above):
@@ -133,9 +151,9 @@
 
 def step_kernel(
     cap,
-    parent,
-    nest,
-    mixing,
+    parent_hbm,
+    nest_hbm,
+    mixing_hbm,
     parent_e,
     parent_n,
     nest_e,
@@ -144,9 +162,14 @@
     strip_block,
     strip_target,
     strip_count,
+    start,
+    halos,
+    nest_coef,
     parent_out,
-    nest_out,
     bulk_out,
+    parent,
+    nest,
+    mixing,
     edges,
     pack_top,
     pack_bottom,
@@ -176,16 +199,22 @@
     rim_out,
     rim_in,
     parent_coef,
-    nest_coef,
     tag_sum,
     tag_in,
-    start,
     halo_out,
     halo_in,
-    halos,
     send_sem,
     recv_sem,
+    load_sem,
 ):
+    loads = [
+        pltpu.make_async_copy(src, dst, load_sem.at[at])
+        for at, (src, dst) in enumerate(
+            ((parent_hbm, parent), (mixing_hbm, mixing), (nest_hbm, nest))
+        )
+    ]
+    for copy in loads:
+        copy.start()
     got = (None, got1, got2, got3, got4)
     route = (None, route1, route2, route3, route4)
     first = cap[0]
@@ -233,8 +262,6 @@
     pack_top[0:3] = nest_e[0:3]
     pack_top[3:6] = nest_n[0:3]
     pack_top[6:8] = parent_n[0:2]
-    edges[0:LEVELS] = mixing[...]
-
     has_above = tile > 0
     has_below = tile < TILES - 1
 
@@ -302,7 +329,10 @@
             near_out[2 * pair + side] = taken[2 * first :, lanes]
         return 0
 
+    loads[0].wait()
     lax.fori_loop(0, LINES // 2, pack, 0)
+    loads[1].wait()
+    edges[0:LEVELS] = mixing[...]
 
     pl.semaphore_wait(barrier, len(peers))
 
@@ -550,6 +580,7 @@
     share(1)
 
     near_copy.wait_recv()
+    loads[2].wait()
 
     def add_blocks(line, taken):
         for c in range(COLS // LANES):
@@ -601,15 +632,21 @@
         rim_in[1] = jnp.zeros((LINES, COLS), F32)
 
     def parent_level(at, _):
-        total = None
+        results = []
         for which in range(2):
             line = which * LEVELS + at
-            result = relax(
-                solved[line], rim_in[0, pl.ds(line, 1), :], rim_in[1, pl.ds(line, 1), :], parent_coef
+            results.append(
+                relax(
+                    halves_of(solved, line),
+                    rim_in[0, pl.ds(line, 1), :],
+                    rim_in[1, pl.ds(line, 1), :],
+                    parent_coef,
+                )
             )
-            parent_out[line] = result
-            total = result if total is None else total + result
-        tag_sum[at] = total
+            for part in range(2):
+                parent_out[line, 8 * part : 8 * part + 8] = results[which][part]
+        for part in range(2):
+            tag_sum[at, 8 * part : 8 * part + 8] = results[0][part] + results[1][part]
         return 0
 
     lax.fori_loop(0, LEVELS, parent_level, 0)
@@ -704,17 +741,6 @@
         third, edge_row, second, e_bottom(0), n_bottom(0), own(nest_n, last)
     )
 
-    def nest_line(line, _):
-        value = start[line]
-        for step in range(NSUB):
-            value = relax(
-                value, halos[0, step, pl.ds(line, 1), :], halos[1, step, pl.ds(line, 1), :], nest_coef
-            )
-        nest_out[line] = value
-        return 0
-
-    lax.fori_loop(0, LINES, nest_line, 0)
-
     for copy, guard in pending:
         if guard is None:
             copy.wait_send()
@@ -722,7 +748,47 @@
             pl.when(guard)(copy.wait_send)
 
 
+def finish_kernel(
+    group, start, halos, coef, parent, bulk, parent_out, nest_out, bulk_out, held, sems
+):
+    copies = [
+        pltpu.make_async_copy(parent, parent_out, sems.at[0]),
+        pltpu.make_async_copy(bulk, bulk_out, sems.at[1]),
+    ]
+    for copy in copies:
+        copy.start()
+
+    def part_copy(at):
+        lines = pl.ds(group * at, group)
+        return pltpu.make_async_copy(held.at[lines], nest_out.at[lines], sems.at[2 + at])
+
+    def lines_at(at, _):
+        lines = [group * at + k for k in range(group)]
+        values = [halves_of(start, line) for line in lines]
+        for step in range(NSUB):
+            for k, line in enumerate(lines):
+                values[k] = relax(
+                    values[k],
+                    halos[0, step, pl.ds(line, 1), :],
+                    halos[1, step, pl.ds(line, 1), :],
+                    coef,
+                )
+        for k, line in enumerate(lines):
+            for part in range(2):
+                held[line, 8 * part : 8 * part + 8] = values[k][part]
+        part_copy(at).start()
+        return 0
+
+    lax.fori_loop(0, LINES // group, lines_at, 0)
+    for copy in copies:
+        copy.wait()
+    for at in range(LINES // group):
+        part_copy(at).wait()
+
+
 VMEM = pl.BlockSpec(memory_space=pltpu.VMEM)
+ANY = pl.BlockSpec(memory_space=pl.ANY)
+GROUP = 4
 SMEM = pl.BlockSpec(memory_space=pltpu.SMEM)
 
 
@@ -731,6 +797,9 @@
     grid = (LINES, ROWS, COLS)
     copies = 3 + 1 + 20 + 8 + 2 + 2 + 4 + 2 + 3 + 2
     shapes = [
+        pltpu.VMEM(grid, F32),
+        pltpu.VMEM(grid, F32),
+        pltpu.VMEM((LEVELS, ROWS, COLS), F32),
         pltpu.VMEM((LEVELS + 1, ROWS, COLS), F32),
         pltpu.VMEM((8, COLS), F32),
         pltpu.VMEM((8, COLS), F32),
@@ -756,25 +825,25 @@
         pltpu.VMEM((2, LINES, COLS), F32),
         pltpu.VMEM((2, LINES, COLS), F32),
         pltpu.VMEM((5, ROWS, COLS), F32),
-        pltpu.VMEM((5, ROWS, COLS), F32),
         pltpu.VMEM((LEVELS, ROWS, COLS), F32),
         pltpu.VMEM((3, LEVELS, ROWS, COLS // 4), F32),
-        pltpu.VMEM(grid, F32),
-        pltpu.VMEM((2, NSUB, LINES, COLS), F32),
         pltpu.VMEM((2, NSUB, LINES, COLS), F32),
         pltpu.VMEM((2, NSUB, LINES, COLS), F32),
         pltpu.SemaphoreType.DMA((copies,)),
         pltpu.SemaphoreType.DMA((copies,)),
+        pltpu.SemaphoreType.DMA((3,)),
     ]
     return pl.pallas_call(
         functools.partial(step_kernel, cap),
         out_shape=[
             jax.ShapeDtypeStruct(grid, F32),
+            jax.ShapeDtypeStruct((2, NSUB, LINES, COLS), F32),
+            jax.ShapeDtypeStruct((5, ROWS, COLS), F32),
             jax.ShapeDtypeStruct(grid, F32),
             jax.ShapeDtypeStruct((LEVELS, ROWS, COLS // 4), F32),
         ],
-        in_specs=[VMEM] * 10 + [SMEM],
-        out_specs=[VMEM] * 3,
+        in_specs=[ANY] * 3 + [VMEM] * 7 + [SMEM],
+        out_specs=[VMEM] * 5,
         scratch_shapes=shapes,
         compiler_params=pltpu.CompilerParams(
             collective_id=collective, has_side_effects=True, vmem_limit_bytes=56 * 1024 * 1024
@@ -816,12 +885,30 @@
         in_specs=[VMEM, SMEM],
         out_specs=SMEM,
     )(strip_tile, strip_count)
-    parent_adjoint, nest_adjoint, bulk_adjoint = lax.cond(
-        flag[0] > 0,
-        lambda *a: step_call(FULL, 1, a),
-        lambda *a: step_call(USUAL, 2, a),
+    states = lax.switch(
+        flag[0],
+        [
+            lambda *a: step_call(SMALL, 3, a),
+            lambda *a: step_call(USUAL, 2, a),
+            lambda *a: step_call(FULL, 1, a),
+        ],
         *arrays,
     )
+    parent_adjoint, nest_adjoint, bulk_adjoint = pl.pallas_call(
+        functools.partial(finish_kernel, GROUP),
+        out_shape=[
+            jax.ShapeDtypeStruct(grid, F32),
+            jax.ShapeDtypeStruct(grid, F32),
+            jax.ShapeDtypeStruct((LEVELS, ROWS, COLS // 4), F32),
+        ],
+        in_specs=[VMEM] * 5,
+        out_specs=[ANY] * 3,
+        scratch_shapes=[
+            pltpu.VMEM(grid, F32),
+            pltpu.SemaphoreType.DMA((2 + LINES // GROUP,)),
+        ],
+        compiler_params=pltpu.CompilerParams(vmem_limit_bytes=32 * 1024 * 1024),
+    )(*states)
     return parent_adjoint.reshape(full_shape), nest_adjoint.reshape(full_shape), bulk_adjoint
 
 

time: 63.8 us -> 57 us (0.89)
  Pallas kernels: 58.3 us -> 54 us
  local copies, waits for them, and re-layouts: 3.96 us -> 1.36 us
    pallas_call x1, Pallas kernels: 55.3 us -> 49.6 us  [step_call(): pl.pallas_call(functools.partial(step_kernel, cap), out_shape=[jax.ShapeD...]
    pallas_call x0 -> x1, Pallas kernels: none -> 2.85 us  [shards(): pl.pallas_call(functools.partial(finish_kernel, GROUP), out_shape=[jax.Sh...]
    unnamed x7 -> x4, local copies, waits for them, and re-layouts: 3.24 us -> 0.64 us
    pallas_call x1, Pallas kernels: 2.96 us -> 1.57 us  [shards(): pl.pallas_call(plan_kernel, out_shape=jax.ShapeDtypeStruct((1,), jnp.int3...]
where the time goes in v2:
time: 57 us; the launch traced here: 56.7 us
  Pallas kernels  54 us (95%)
  local copies, waits for them, and re-layouts  1.36 us (2%)
  between operations  1.32 us (2%)
    pallas_call x1, Pallas kernels, step_call(): pl.pallas_call(functools.partial(step_kernel, cap), out_shape=[jax.ShapeD...  49.6 us
    pallas_call x1, Pallas kernels, shards(): pl.pallas_call(functools.partial(finish_kernel, GROUP), out_shape=[jax.Sh...  2.85 us
    pallas_call x1, Pallas kernels, shards(): pl.pallas_call(plan_kernel, out_shape=jax.ShapeDtypeStruct((1,), jnp.int3...  1.57 us

profile of v2, /device:TPU:1, one launch (start us, length us, event | category | flops | bytes accessed | tf_op | source)
XLA Modules:
  0.0 56.7 jit_solution(472063661416382542)
XLA Ops:
  0.6 0.0 copy-start
  0.6 1.6 %shard_map.130 = s32[1]{0:T(128)} custom-call(s32[16,256]{1,0:T(8,128)} %tile_ref.1, s32[16]{0:T(128)} %count_ref.1), custom_call_target="tpu_custom_call" | custom-call | tf_op jit(solution)/shard_map/pallas_call | solution.py:882
  2.9 0.0 copy-start.4
  2.9 0.0 copy-done
  2.9 0.6 %copy-done.4 = s32[16]{0:T(128)S(1)} copy-done((s32[16]{0:T(128)S(1)}, s32[16]{0:T(128)}, u32[]{:S(2)}) %copy-start.4) | copy-done | bytes 88
  3.5 50.3 %conditional.1 = ((f32[16,16,1024]{2,1,0:T(8,128)S(1)}, f32[2,3,16,1024]{3,2,1,0:T(8,128)S(1)}, f32[5,16,1024]{2,1,0:T(8,128)S(1)}, f32[16,16,1024]{2,1,0:T(8,128)S(1)}, f32[8,16,256]{2,1,0:T(8,128)S(1)})) conditional(s32[]{:T(128)} %bitcast, (f32[16,16,1024]{2,1,0:T(8,128)}, f32[16,16,1024]{2,1,0:T(8,128)}, ...), branch_computations={%region_0.0_spmd, %region_1.0_spmd, %region_2.0_spmd} | conditional | bytes 65572 | solution.py:888
  3.5 0.0 copy-start.2
  3.5 0.7 %copy-done.2 = s32[16,256]{1,0:T(8,128)S(1)} copy-done((s32[16,256]{1,0:T(8,128)S(1)}, s32[16,256]{1,0:T(8,128)}, u32[]{:S(2)}) %copy-start.2) | copy-done | bytes 16408 | tf_op jit(solution)/shard_map/cond
  4.2 49.6 %branch_1_fun.1 = (f32[16,16,1024]{2,1,0:T(8,128)S(1)}, f32[2,3,16,1024]{3,2,1,0:T(8,128)S(1)}, f32[5,16,1024]{2,1,0:T(8,128)S(1)}, f32[16,16,1024]{2,1,0:T(8,128)S(1)}, f32[8,16,256]{2,1,0:T(8,128)S(1)}) custom-call(f32[16,16,1024]{2,1,0:T(8,128)} %get-tuple-element.77.parent_hbm, f32[16,16,1024]{2,1,0:T(8,128)} %get-tuple-element.78.nest_hbm, ...), custom_call_target="tpu_custom_call" | custom-call | tf_op jit(solution)/shard_map/cond/branch_1_fun/pallas_call | solution.py:836
  53.9 2.8 %shard_map.131 = (f32[16,16,1024]{2,1,0:T(8,128)}, f32[16,16,1024]{2,1,0:T(8,128)}, f32[8,16,256]{2,1,0:T(8,128)}) custom-call(f32[16,16,1024]{2,1,0:T(8,128)S(1)} %get-tuple-element.110.start, f32[2,3,16,1024]{3,2,1,0:T(8,128)S(1)} %get-tuple-element.111.halos, f32[5,16,1024]{2,1,0:T(8,128)S(1)} %get-tuple-element.112.coef, ...), custom_call_target="tpu_custom_call" | custom-call | tf_op jit(solution)/shard_map/pallas_call | solution.py:897
Async XLA Ops:
  0.6 2.2 %copy-start = (s32[16,256]{1,0:T(8,128)S(1)}, s32[16,256]{1,0:T(8,128)}, u32[]{:S(2)}) copy-start(s32[16,256]{1,0:T(8,128)} %tile_ref.1) | copy-start | bytes 49156
  2.9 0.7 %copy-start.4 = (s32[16]{0:T(128)S(1)}, s32[16]{0:T(128)}, u32[]{:S(2)}) copy-start(s32[16]{0:T(128)} %count_ref.1) | copy-start | bytes 196
  3.5 0.7 %copy-start.2 = (s32[16,256]{1,0:T(8,128)S(1)}, s32[16,256]{1,0:T(8,128)}, u32[]{:S(2)}) copy-start(s32[16,256]{1,0:T(8,128)} %get-tuple-element.85.strip_block) | copy-start | bytes 49156 | tf_op jit(solution)/shard_map/cond

commit v3 on v2

--- a/solution.py
+++ b/solution.py
@@ -54,9 +54,10 @@
     return total
 
 
-def plan_kernel(tile_ref, count_ref, flag_ref):
+def plan_kernel(tile_ref, count_ref, flag_ref, listed_ref):
     live = iota((TILES, ENTRIES), 1) < counts_column(count_ref)
     listed = jnp.where(live, tile_ref[...], -1)
+    listed_ref[...] = listed
     lane = iota((TILES, LANES), 1)
     count = jnp.zeros((TILES, LANES), F32)
     for source in range(TILES):
@@ -154,14 +155,13 @@
     parent_hbm,
     nest_hbm,
     mixing_hbm,
-    parent_e,
-    parent_n,
-    nest_e,
-    nest_n,
-    strip_tile,
-    strip_block,
-    strip_target,
-    strip_count,
+    parent_e_hbm,
+    parent_n_hbm,
+    nest_e_hbm,
+    nest_n_hbm,
+    block_hbm,
+    target_hbm,
+    listed_hbm,
     start,
     halos,
     nest_coef,
@@ -170,6 +170,13 @@
     parent,
     nest,
     mixing,
+    parent_e,
+    parent_n,
+    nest_e,
+    nest_n,
+    strip_block,
+    strip_target,
+    strip_listed,
     edges,
     pack_top,
     pack_bottom,
@@ -210,7 +217,18 @@
     loads = [
         pltpu.make_async_copy(src, dst, load_sem.at[at])
         for at, (src, dst) in enumerate(
-            ((parent_hbm, parent), (mixing_hbm, mixing), (nest_hbm, nest))
+            (
+                (listed_hbm, strip_listed),
+                (block_hbm, strip_block),
+                (parent_hbm, parent),
+                (mixing_hbm, mixing),
+                (nest_e_hbm, nest_e),
+                (nest_n_hbm, nest_n),
+                (parent_n_hbm, parent_n),
+                (parent_e_hbm, parent_e),
+                (target_hbm, strip_target),
+                (nest_hbm, nest),
+            )
         )
     ]
     for copy in loads:
@@ -255,20 +273,13 @@
         pending.append((copy, guard))
         return copy
 
-    pack_bottom[0:3] = nest_e[ROWS - 3 : ROWS]
-    pack_bottom[3:6] = nest_n[ROWS - 3 : ROWS]
-    pack_bottom[6:7] = parent_n[ROWS - 1 : ROWS]
-    pack_bottom[7:8] = parent_n[ROWS - 1 : ROWS]
-    pack_top[0:3] = nest_e[0:3]
-    pack_top[3:6] = nest_n[0:3]
-    pack_top[6:8] = parent_n[0:2]
     has_above = tile > 0
     has_below = tile < TILES - 1
 
+    loads[0].wait()
+    loads[1].wait()
     row = iota((TILES, ENTRIES), 0)
-    entry = iota((TILES, ENTRIES), 1)
-    live = entry < counts_column(strip_count)
-    listed = jnp.where(live, strip_tile[...], -1)
+    listed = strip_listed[...]
     mine = jnp.where(listed == tile, 1.0, 0.0)
     upto = jnp.where(
         iota((ENTRIES, ENTRIES), 0) <= iota((ENTRIES, ENTRIES), 1), 1.0, 0.0
@@ -329,10 +340,19 @@
             near_out[2 * pair + side] = taken[2 * first :, lanes]
         return 0
 
-    loads[0].wait()
+    loads[2].wait()
     lax.fori_loop(0, LINES // 2, pack, 0)
-    loads[1].wait()
+    for copy in loads[3:7]:
+        copy.wait()
     edges[0:LEVELS] = mixing[...]
+
+    pack_bottom[0:3] = nest_e[ROWS - 3 : ROWS]
+    pack_bottom[3:6] = nest_n[ROWS - 3 : ROWS]
+    pack_bottom[6:7] = parent_n[ROWS - 1 : ROWS]
+    pack_bottom[7:8] = parent_n[ROWS - 1 : ROWS]
+    pack_top[0:3] = nest_e[0:3]
+    pack_top[3:6] = nest_n[0:3]
+    pack_top[6:8] = parent_n[0:2]
 
     pl.semaphore_wait(barrier, len(peers))
 
@@ -444,9 +464,9 @@
             sweep(rows, 1.0 + edges[at + down, rows, :], field(0, at, rows), field(1, at, rows))
             outer_copy[part].start()
 
-    own_tiles = strip_tile[pl.ds(tile, 1), :]
-    own_live = iota((1, ENTRIES), 1) < strip_count[tile]
-    own_tiles = jnp.where(own_live, own_tiles, -1)
+    for copy in loads[7:]:
+        copy.wait()
+    own_tiles = strip_listed[pl.ds(tile, 1), :]
     source_row = iota((TILES, ENTRIES), 0)
     from_source = jnp.where(own_tiles == source_row, 1.0, 0.0)
     own_rank = jnp.sum(
@@ -580,7 +600,6 @@
     share(1)
 
     near_copy.wait_recv()
-    loads[2].wait()
 
     def add_blocks(line, taken):
         for c in range(COLS // LANES):
@@ -800,6 +819,13 @@
         pltpu.VMEM(grid, F32),
         pltpu.VMEM(grid, F32),
         pltpu.VMEM((LEVELS, ROWS, COLS), F32),
+        pltpu.VMEM((ROWS, COLS), F32),
+        pltpu.VMEM((ROWS, COLS), F32),
+        pltpu.VMEM((ROWS, COLS), F32),
+        pltpu.VMEM((ROWS, COLS), F32),
+        pltpu.VMEM((TILES, ENTRIES), jnp.int32),
+        pltpu.VMEM((TILES, ENTRIES), jnp.int32),
+        pltpu.VMEM((TILES, ENTRIES), jnp.int32),
         pltpu.VMEM((LEVELS + 1, ROWS, COLS), F32),
         pltpu.VMEM((8, COLS), F32),
         pltpu.VMEM((8, COLS), F32),
@@ -831,7 +857,7 @@
         pltpu.VMEM((2, NSUB, LINES, COLS), F32),
         pltpu.SemaphoreType.DMA((copies,)),
         pltpu.SemaphoreType.DMA((copies,)),
-        pltpu.SemaphoreType.DMA((3,)),
+        pltpu.SemaphoreType.DMA((10,)),
     ]
     return pl.pallas_call(
         functools.partial(step_kernel, cap),
@@ -842,7 +868,7 @@
             jax.ShapeDtypeStruct(grid, F32),
             jax.ShapeDtypeStruct((LEVELS, ROWS, COLS // 4), F32),
         ],
-        in_specs=[ANY] * 3 + [VMEM] * 7 + [SMEM],
+        in_specs=[ANY] * 10,
         out_specs=[VMEM] * 5,
         scratch_shapes=shapes,
         compiler_params=pltpu.CompilerParams(
@@ -866,6 +892,15 @@
 ):
     full_shape = parent_field.shape
     grid = (LINES, ROWS, COLS)
+    flag, strip_listed = pl.pallas_call(
+        plan_kernel,
+        out_shape=[
+            jax.ShapeDtypeStruct((1,), jnp.int32),
+            jax.ShapeDtypeStruct((TILES, ENTRIES), jnp.int32),
+        ],
+        in_specs=[VMEM, SMEM],
+        out_specs=[SMEM, VMEM],
+    )(strip_tile, strip_count)
     arrays = (
         parent_field.reshape(grid),
         nest_field.reshape(grid),
@@ -874,17 +909,10 @@
         parent_northward,
         nest_eastward,
         nest_northward,
-        strip_tile,
         strip_block,
         strip_target,
-        strip_count,
-    )
-    flag = pl.pallas_call(
-        plan_kernel,
-        out_shape=jax.ShapeDtypeStruct((1,), jnp.int32),
-        in_specs=[VMEM, SMEM],
-        out_specs=SMEM,
-    )(strip_tile, strip_count)
+        strip_listed,
+    )
     states = lax.switch(
         flag[0],
         [

time: 57 us -> 52.9 us (0.928)
  Pallas kernels: 54 us -> 50.6 us
  local copies, waits for them, and re-layouts: 1.36 us -> 0.72 us
    pallas_call x1, Pallas kernels: 49.6 us -> 46.2 us  [step_call(): pl.pallas_call(functools.partial(step_kernel, cap), out_shape=[jax.ShapeD...]
    unnamed x4 -> x2, local copies, waits for them, and re-layouts: 0.64 us -> 0.01 us
where the time goes in v3:
time: 52.9 us; the launch traced here: 52.7 us
  Pallas kernels  50.6 us (96%)
  between operations  1.31 us (2%)
  local copies, waits for them, and re-layouts  0.72 us (1%)
    pallas_call x1, Pallas kernels, step_call(): pl.pallas_call(functools.partial(step_kernel, cap), out_shape=[jax.ShapeD...  46.2 us
    pallas_call x1, Pallas kernels, shards(): pl.pallas_call(functools.partial(finish_kernel, GROUP), out_shape=[jax.Sh...  2.85 us
    pallas_call x1, Pallas kernels, shards(): pl.pallas_call(plan_kernel, out_shape=[jax.ShapeDtypeStruct((1,), jnp.int...  1.57 us

profile of v3, /device:TPU:1, one launch (start us, length us, event | category | flops | bytes accessed | tf_op | source)
XLA Modules:
  0.0 52.7 jit_solution(517514992512899211)
XLA Ops:
  0.6 0.0 copy-start
  0.6 1.6 %shard_map.130 = (s32[1]{0:T(128)}, s32[16,256]{1,0:T(8,128)S(1)}) custom-call(s32[16,256]{1,0:T(8,128)} %tile_ref.1, s32[16]{0:T(128)} %count_ref.1), custom_call_target="tpu_custom_call" | custom-call | tf_op jit(solution)/shard_map/pallas_call | solution.py:895
  2.9 0.0 copy-done
  2.9 46.9 %conditional.1 = ((f32[16,16,1024]{2,1,0:T(8,128)S(1)}, f32[2,3,16,1024]{3,2,1,0:T(8,128)S(1)}, f32[5,16,1024]{2,1,0:T(8,128)S(1)}, f32[16,16,1024]{2,1,0:T(8,128)S(1)}, f32[8,16,256]{2,1,0:T(8,128)S(1)})) conditional(s32[]{:T(128)} %bitcast, (f32[16,16,1024]{2,1,0:T(8,128)}, f32[16,16,1024]{2,1,0:T(8,128)}, ...), branch_computations={%region_0.0_spmd, %region_1.0_spmd, %region_2.0_spmd} | conditional | bytes 65572 | solution.py:916
  2.9 0.0 copy-start.1
  2.9 0.7 %copy-done.1 = s32[16,256]{1,0:T(8,128)S(1)} copy-done((s32[16,256]{1,0:T(8,128)S(1)}, s32[16,256]{1,0:T(8,128)}, u32[]{:S(2)}) %copy-start.1) | copy-done | bytes 16408 | tf_op jit(solution)/shard_map/cond
  3.6 46.2 %branch_0_fun.1 = (f32[16,16,1024]{2,1,0:T(8,128)S(1)}, f32[2,3,16,1024]{3,2,1,0:T(8,128)S(1)}, f32[5,16,1024]{2,1,0:T(8,128)S(1)}, f32[16,16,1024]{2,1,0:T(8,128)S(1)}, f32[8,16,256]{2,1,0:T(8,128)S(1)}) custom-call(f32[16,16,1024]{2,1,0:T(8,128)} %get-tuple-element.60.parent_hbm, f32[16,16,1024]{2,1,0:T(8,128)} %get-tuple-element.61.nest_hbm, ...), custom_call_target="tpu_custom_call" | custom-call | tf_op jit(solution)/shard_map/cond/branch_0_fun/pallas_call | solution.py:862
  49.8 2.8 %shard_map.131 = (f32[16,16,1024]{2,1,0:T(8,128)}, f32[16,16,1024]{2,1,0:T(8,128)}, f32[8,16,256]{2,1,0:T(8,128)}) custom-call(f32[16,16,1024]{2,1,0:T(8,128)S(1)} %get-tuple-element.105.start, f32[2,3,16,1024]{3,2,1,0:T(8,128)S(1)} %get-tuple-element.106.halos, f32[5,16,1024]{2,1,0:T(8,128)S(1)} %get-tuple-element.107.coef, ...), custom_call_target="tpu_custom_call" | custom-call | tf_op jit(solution)/shard_map/pallas_call | solution.py:925
Async XLA Ops:
  0.6 2.2 %copy-start = (s32[16,256]{1,0:T(8,128)S(1)}, s32[16,256]{1,0:T(8,128)}, u32[]{:S(2)}) copy-start(s32[16,256]{1,0:T(8,128)} %param.22) | copy-start | bytes 49156
  2.9 0.7 %copy-start.1 = (s32[16,256]{1,0:T(8,128)S(1)}, s32[16,256]{1,0:T(8,128)}, u32[]{:S(2)}) copy-start(s32[16,256]{1,0:T(8,128)} %get-tuple-element.68.target_hbm) | copy-start | bytes 49156 | tf_op jit(solution)/shard_map/cond

commit v4 on v3

--- a/solution.py
+++ b/solution.py
@@ -21,6 +21,8 @@
 NBLK = 128
 ENTRIES = 256
 NSUB = 3
+HALF = LINES // 2
+PARTS = 1
 FULL = (112, 80, 48, 16)
 USUAL = (64, 48, 40, 16)
 SMALL = (56, 40, 32, 16)
@@ -132,7 +134,7 @@
 
 
 def relax_row(x, above, below, eastward, northward, north_above):
-    wide = (LINES, COLS)
+    wide = x.shape
     center, north, north_up, east, west = coefficients(
         jnp.broadcast_to(eastward, (8, COLS)),
         jnp.broadcast_to(northward, (8, COLS)),
@@ -317,11 +319,10 @@
     def gather_matrix(begin, size):
         wanted = (iota((size, ENTRIES), 0) + begin).astype(F32)
 
-        def one(nest_tile, total):
-            at = pl.ds(nest_tile, 1)
-            return total + jnp.where(slot_of[at, :] == wanted, block_of[at, :], 0.0)
-
-        total = lax.fori_loop(0, TILES, one, jnp.zeros((size, ENTRIES), F32))
+        total = jnp.zeros((size, ENTRIES), F32)
+        for nest_tile in range(TILES):
+            at = slice(nest_tile, nest_tile + 1)
+            total = jnp.where(slot_of[at, :] == wanted, block_of[at, :], total)
         index = jnp.sum(total, axis=1, keepdims=True) - 1.0
         return jnp.where(index == iota((size, NBLK), 1).astype(F32), 1.0, 0.0).astype(BF16)
 
@@ -330,7 +331,15 @@
         axis=0,
     )
 
-    def pack(pair, _):
+    def lines_of(part):
+        return pl.ds(HALF * part, HALF)
+
+    def pack(quad, _):
+        for pair in (2 * quad, 2 * quad + 1):
+            pack_pair(pair)
+        return 0
+
+    def pack_pair(pair):
         cells = jnp.concatenate([blocks_of(parent, 2 * pair), blocks_of(parent, 2 * pair + 1)], axis=1)
         taken = routed(gather, cells)
         for side in range(2):
@@ -338,66 +347,37 @@
             outgoing[0, 2 * pair + side] = taken[:first, lanes]
             outgoing[1, 2 * pair + side] = taken[first : 2 * first, lanes]
             near_out[2 * pair + side] = taken[2 * first :, lanes]
-        return 0
-
-    loads[2].wait()
-    lax.fori_loop(0, LINES // 2, pack, 0)
-    for copy in loads[3:7]:
-        copy.wait()
-    edges[0:LEVELS] = mixing[...]
-
-    pack_bottom[0:3] = nest_e[ROWS - 3 : ROWS]
-    pack_bottom[3:6] = nest_n[ROWS - 3 : ROWS]
-    pack_bottom[6:7] = parent_n[ROWS - 1 : ROWS]
-    pack_bottom[7:8] = parent_n[ROWS - 1 : ROWS]
-    pack_top[0:3] = nest_e[0:3]
-    pack_top[3:6] = nest_n[0:3]
-    pack_top[6:8] = parent_n[0:2]
-
-    pl.semaphore_wait(barrier, len(peers))
-
-    edge_copy = remote(edges.at[0], edges.at[LEVELS], {"lev": (lev + 3) % 4}, lev > 0)
-    pl.when(lev > 0)(edge_copy.start)
-    pack_down_copy = remote(pack_bottom, coef_top, {"tile": tile_up}, has_below)
-    pl.when(has_below)(pack_down_copy.start)
-    pack_up_copy = remote(pack_top, coef_bottom, {"tile": tile_down}, has_above)
-    pl.when(has_above)(pack_up_copy.start)
-
-    near_copy = remote(near_out, near_in, {"tile": sibling})
-    near_copy.start()
+
     cuts = (0, cap[3], cap[2], cap[1], cap[0])
     hop_copy = {}
-    for hop in range(1, 5):
-        for piece in range(5 - hop):
+    side_copy = {}
+    for part in range(PARTS):
+        lines = pl.ds(LINES // PARTS * part, LINES // PARTS)
+        for hop in range(1, 5):
+            src = outgoing if hop == 1 else got[hop - 1]
             for way in range(2):
-                part = pl.ds(cuts[piece], cuts[piece + 1] - cuts[piece])
-                src = outgoing if hop == 1 else got[hop - 1]
-                hop_copy[hop, piece, way] = remote(
-                    src.at[way, :, part, :], got[hop].at[way, :, part, :], {"tile": ring[way]}
+                for piece in range(5 - hop):
+                    slots = pl.ds(cuts[piece], cuts[piece + 1] - cuts[piece])
+                    hop_copy[hop, piece, way, part] = remote(
+                        src.at[way, lines, slots, :],
+                        got[hop].at[way, lines, slots, :],
+                        {"tile": ring[way]},
+                    )
+                side_copy[hop, way, part] = remote(
+                    got[hop].at[way, lines], got[hop].at[2 + way, lines], {"tile": sibling}
                 )
-    side_copy = {}
-    for hop in range(1, 5):
-        for way in range(2):
-            side_copy[hop, way] = remote(got[hop].at[way], got[hop].at[2 + way], {"tile": sibling})
-    for piece in range(4):
-        for way in range(2):
-            hop_copy[1, piece, way].start()
-
-    def relay(hop, piece):
-        for way in range(2):
-            hop_copy[hop - 1, piece, way].wait_recv()
-            hop_copy[hop, piece, way].start()
-
-    def share(hop):
-        for way in range(2):
-            hop_copy[hop, 4 - hop, way].wait_recv()
-            side_copy[hop, way].start()
-
-    pl.when(lev < 3)(edge_copy.wait_recv)
-
-    @pl.when(lev == 3)
-    def _():
-        edges[LEVELS] = jnp.zeros((ROWS, COLS), F32)
+
+    def send(part):
+        for piece in range(4):
+            for way in range(2):
+                hop_copy[1, piece, way, part].start()
+
+    loads[2].wait()
+    for part in range(PARTS):
+        lax.fori_loop(HALF // 2 // PARTS * part, HALF // 2 // PARTS * (part + 1), pack, 0)
+        if part == 0:
+            pl.semaphore_wait(barrier, len(peers))
+        send(part)
 
     def level(step):
         return step + down * (LEVELS - 1 - 2 * step)
@@ -406,7 +386,7 @@
         return parent[which * LEVELS + at, rows, :]
 
     def sweep(rows, pivot, value0, value1):
-        for step in range(LEVELS):
+        for step in range(LEVELS - 1):
             at = level(step)
             edge = edges[at + 1 - down, rows, :]
             inverse = 1.0 / (pivot + edge)
@@ -416,17 +396,19 @@
             solved[at, rows, :] = carry0
             solved[LEVELS + at, rows, :] = carry1
             weight[at, rows, :] = ratio
-            if step < LEVELS - 1:
-                follow = level(step + 1)
-                pivot = 1.0 + ratio * pivot
-                value0 = field(0, follow, rows) + edge * carry0
-                value1 = field(1, follow, rows) + edge * carry1
+            follow = level(step + 1)
+            pivot = 1.0 + ratio * pivot
+            value0 = field(0, follow, rows) + edge * carry0
+            value1 = field(1, follow, rows) + edge * carry1
         message[0, rows, :] = pivot
         message[1, rows, :] = value0
         message[2, rows, :] = value1
 
-    def back(rows, value0, value1, last):
-        for step in range(last, -1, -1):
+    def back(rows, value0, value1):
+        at = level(LEVELS - 1)
+        solved[at, rows, :] = value0
+        solved[LEVELS + at, rows, :] = value1
+        for step in range(LEVELS - 2, -1, -1):
             at = level(step)
             ratio = weight[at, rows, :]
             value0 = solved[at, rows, :] + ratio * value0
@@ -457,12 +439,54 @@
         for rows in halves
     ]
 
+    for copy in loads[3:4]:
+        copy.wait()
+    edges[0:LEVELS] = mixing[...]
+
+    @pl.when(lev == 3)
+    def _():
+        edges[LEVELS] = jnp.zeros((ROWS, COLS), F32)
+
+    edge_copy = remote(edges.at[0], edges.at[LEVELS], {"lev": (lev + 3) % 4}, lev > 0)
+    pl.when(lev > 0)(edge_copy.start)
+
     @pl.when(outer)
     def _():
         for part, rows in enumerate(halves):
             at = level(0)
             sweep(rows, 1.0 + edges[at + down, rows, :], field(0, at, rows), field(1, at, rows))
             outer_copy[part].start()
+
+    for copy in loads[4:7]:
+        copy.wait()
+
+    pack_bottom[0:3] = nest_e[ROWS - 3 : ROWS]
+    pack_bottom[3:6] = nest_n[ROWS - 3 : ROWS]
+    pack_bottom[6:7] = parent_n[ROWS - 1 : ROWS]
+    pack_bottom[7:8] = parent_n[ROWS - 1 : ROWS]
+    pack_top[0:3] = nest_e[0:3]
+    pack_top[3:6] = nest_n[0:3]
+    pack_top[6:8] = parent_n[0:2]
+
+    pack_down_copy = remote(pack_bottom, coef_top, {"tile": tile_up}, has_below)
+    pl.when(has_below)(pack_down_copy.start)
+    pack_up_copy = remote(pack_top, coef_bottom, {"tile": tile_down}, has_above)
+    pl.when(has_above)(pack_up_copy.start)
+    near_copy = remote(near_out, near_in, {"tile": sibling})
+    near_copy.start()
+
+    def relay(hop, *pieces):
+        for part in range(PARTS):
+            for piece in pieces:
+                for way in range(2):
+                    hop_copy[hop - 1, piece, way, part].wait_recv()
+                    hop_copy[hop, piece, way, part].start()
+
+    def share(hop):
+        for part in range(PARTS):
+            for way in range(2):
+                hop_copy[hop, 4 - hop, way, part].wait_recv()
+                side_copy[hop, way, part].start()
 
     for copy in loads[7:]:
         copy.wait()
@@ -517,6 +541,8 @@
     own_blocks = strip_block[pl.ds(tile, 1), :]
     own_blocks = jnp.where(own_tiles == tile, (own_blocks & 7) * ROWS + (own_blocks >> 3), -1)
     route_own[...] = onehot_product(lands, picks(own_blocks.astype(F32), NBLK)).astype(BF16)
+
+    pl.when(lev < 3)(edge_copy.wait_recv)
 
     @pl.when(inner)
     def _():
@@ -534,8 +560,7 @@
             )
             center_copy[part].start()
 
-    relay(2, 0)
-    relay(2, 1)
+    relay(2, 0, 1)
 
     @pl.when(inner)
     def _():
@@ -548,9 +573,7 @@
             inverse = 1.0 / (message[0, rows, :] + ratio * pivot)
             value0 = (message[1, rows, :] + ratio * from_center[1, rows, :]) * inverse
             value1 = (message[2, rows, :] + ratio * from_center[2, rows, :]) * inverse
-            solved[at, rows, :] = value0
-            solved[LEVELS + at, rows, :] = value1
-            back(rows, value0, value1, LEVELS - 2)
+            back(rows, value0, value1)
             for copy in inner_copy[part]:
                 copy.start()
 
@@ -587,7 +610,13 @@
         for part, rows in enumerate(halves):
             for copy in inner_copy[part]:
                 copy.wait_recv()
-            back(rows, from_inner[0, rows, :], from_inner[1, rows, :], LEVELS - 1)
+            edge = edges[level(LEVELS - 1) + 1 - down, rows, :]
+            inverse = 1.0 / (message[0, rows, :] + edge)
+            back(
+                rows,
+                (message[1, rows, :] + edge * from_inner[0, rows, :]) * inverse,
+                (message[2, rows, :] + edge * from_inner[1, rows, :]) * inverse,
+            )
 
     for line in range(LINES):
         rim_out[0, line : line + 1] = solved[line, 0:1, :]
@@ -617,11 +646,17 @@
 
     lax.fori_loop(0, LINES // 2, scatter_near, 0)
 
-    def scatter(hop):
-        for way in range(2):
-            side_copy[hop, way].wait_recv()
-
-        def one(pair, _):
+    def scatter(hop, part):
+        if part < PARTS:
+            for way in range(2):
+                side_copy[hop, way, part].wait_recv()
+
+        def one(quad, _):
+            for pair in (2 * quad, 2 * quad + 1):
+                one_pair(pair)
+            return 0
+
+        def one_pair(pair):
             cells = jnp.concatenate(
                 [
                     jnp.concatenate([got[hop][g, 2 * pair + side] for g in range(4)], axis=0)
@@ -632,13 +667,16 @@
             taken = routed(route[hop][...], cells)
             for side in range(2):
                 add_blocks(2 * pair + side, taken[:, LANES * side : LANES * (side + 1)])
-            return 0
-
-        lax.fori_loop(0, LINES // 2, one, 0)
-
-    relay(3, 0)
-    relay(3, 1)
-
+
+        lax.fori_loop(HALF // 4 * part, HALF // 4 * (part + 1), one, 0)
+
+    relay(3, 0, 1)
+
+    share(2)
+    scatter(1, 0)
+    scatter(1, 1)
+    relay(4, 0)
+    share(3)
     pl.when(has_above)(rim_down.wait_recv)
     pl.when(has_below)(rim_up.wait_recv)
 
@@ -682,83 +720,110 @@
         copy.start()
         tag_copy.append(copy)
 
-    share(2)
-    scatter(1)
-    relay(4, 0)
-    share(3)
-    scatter(2)
+    halo_up = []
+    halo_down = []
+    for part in range(2):
+        lines = lines_of(part)
+        halo_up.append(
+            remote(
+                halo_out.at[0, :, lines, :],
+                halo_in.at[1, :, lines, :],
+                {"tile": tile_down},
+                has_above,
+            )
+        )
+        halo_down.append(
+            remote(
+                halo_out.at[1, :, lines, :],
+                halo_in.at[0, :, lines, :],
+                {"tile": tile_up},
+                has_below,
+            )
+        )
+
+    def send_halo(part):
+        for line in range(HALF * part, HALF * (part + 1)):
+            for r in range(NSUB):
+                halo_out[0, r, line : line + 1] = start[line, r : r + 1, :]
+                at = ROWS - NSUB + r
+                halo_out[1, r, line : line + 1] = start[line, at : at + 1, :]
+        pl.when(has_above)(halo_up[part].start)
+        pl.when(has_below)(halo_down[part].start)
+
+    in_grid = jnp.where(has_below, 1.0, 0.0)
+
+    def e_top(r):
+        return coef_top[r : r + 1]
+
+    def n_top(r):
+        return coef_top[3 + r : 4 + r]
+
+    def e_bottom(r):
+        return coef_bottom[r : r + 1]
+
+    def n_bottom(r):
+        return coef_bottom[3 + r : 4 + r]
+
+    def own(ref, r):
+        return ref[r : r + 1]
+
+    def receive_halo(part):
+        lines = slice(HALF * part, HALF * (part + 1))
+        pl.when(has_above)(halo_down[part].wait_recv)
+        pl.when(has_below)(halo_up[part].wait_recv)
+
+        @pl.when(tile == 0)
+        def _():
+            halo_in[0, :, lines] = jnp.zeros((NSUB, HALF, COLS), F32)
+
+        @pl.when(tile == TILES - 1)
+        def _():
+            halo_in[1, :, lines] = jnp.zeros((NSUB, HALF, COLS), F32)
+
+        far, mid, close = (halo_in[0, r, lines] for r in range(3))
+        inner0, inner1 = (halo_out[0, r, lines] for r in range(2))
+        second = relax_row(mid, far, close, e_top(1), n_top(1), n_top(0))
+        third = relax_row(close, mid, inner0, e_top(2), n_top(2), n_top(1))
+        edge_row = relax_row(inner0, close, inner1, own(nest_e, 0), own(nest_n, 0), n_top(2))
+        halos[0, 0, lines] = close
+        halos[0, 1, lines] = third
+        halos[0, 2, lines] = relax_row(third, second, edge_row, e_top(2), n_top(2), n_top(1))
+        last = ROWS - 1
+        close, mid, far = (halo_in[1, r, lines] for r in range(3))
+        inner1, inner0 = (halo_out[1, r, lines] for r in (1, 2))
+        second = relax_row(mid, close, far, e_bottom(1), n_bottom(1), n_bottom(0))
+        third = in_grid * relax_row(
+            close, inner0, mid, e_bottom(0), n_bottom(0), own(nest_n, last)
+        )
+        edge_row = relax_row(
+            inner0, inner1, close, own(nest_e, last), own(nest_n, last), own(nest_n, last - 1)
+        )
+        halos[1, 0, lines] = close
+        halos[1, 1, lines] = third
+        halos[1, 2, lines] = in_grid * relax_row(
+            third, edge_row, second, e_bottom(0), n_bottom(0), own(nest_n, last)
+        )
+
+    scatter(2, 0)
+    scatter(2, 1)
+    share(4)
+    scatter(3, 0)
+    scatter(4, 0)
+    send_halo(0)
+    scatter(3, 1)
+    scatter(4, 1)
+    send_halo(1)
+    receive_halo(0)
+
+    def first_lines(at, _):
+        sub_steps(start, [GROUP * at + k for k in range(GROUP)], start, halos, nest_coef)
+        return 0
+
+    lax.fori_loop(0, HALF // GROUP, first_lines, 0)
     for copy in tag_copy:
         copy.wait_recv()
     bulk_out[...] = tag_sum[:, :, columns(tag)] + tag_in[0] + tag_in[1] + tag_in[2]
-    share(4)
-    scatter(3)
-    scatter(4)
-
-    for line in range(LINES):
-        for r in range(NSUB):
-            halo_out[0, r, line : line + 1] = start[line, r : r + 1, :]
-            at = ROWS - NSUB + r
-            halo_out[1, r, line : line + 1] = start[line, at : at + 1, :]
-    halo_up = remote(halo_out.at[0], halo_in.at[1], {"tile": tile_down}, has_above)
-    halo_down = remote(halo_out.at[1], halo_in.at[0], {"tile": tile_up}, has_below)
-    pl.when(has_above)(halo_up.start)
-    pl.when(has_below)(halo_down.start)
-    pl.when(has_above)(halo_down.wait_recv)
-    pl.when(has_below)(halo_up.wait_recv)
-
-    @pl.when(tile == 0)
-    def _():
-        halo_in[0] = jnp.zeros((NSUB, LINES, COLS), F32)
-
-    @pl.when(tile == TILES - 1)
-    def _():
-        halo_in[1] = jnp.zeros((NSUB, LINES, COLS), F32)
-
-    in_grid = jnp.where(has_below, 1.0, 0.0)
-
-    def e_top(r):
-        return coef_top[r : r + 1]
-
-    def n_top(r):
-        return coef_top[3 + r : 4 + r]
-
-    def e_bottom(r):
-        return coef_bottom[r : r + 1]
-
-    def n_bottom(r):
-        return coef_bottom[3 + r : 4 + r]
-
-    def own(ref, r):
-        return ref[r : r + 1]
-
-    second = relax_row(halo_in[0, 1], halo_in[0, 0], halo_in[0, 2], e_top(1), n_top(1), n_top(0))
-    third = relax_row(halo_in[0, 2], halo_in[0, 1], halo_out[0, 0], e_top(2), n_top(2), n_top(1))
-    edge_row = relax_row(
-        halo_out[0, 0], halo_in[0, 2], halo_out[0, 1], own(nest_e, 0), own(nest_n, 0), n_top(2)
-    )
-    halos[0, 0] = halo_in[0, 2]
-    halos[0, 1] = third
-    halos[0, 2] = relax_row(third, second, edge_row, e_top(2), n_top(2), n_top(1))
-    last = ROWS - 1
-    second = relax_row(
-        halo_in[1, 1], halo_in[1, 0], halo_in[1, 2], e_bottom(1), n_bottom(1), n_bottom(0)
-    )
-    third = in_grid * relax_row(
-        halo_in[1, 0], halo_out[1, 2], halo_in[1, 1], e_bottom(0), n_bottom(0), own(nest_n, last)
-    )
-    edge_row = relax_row(
-        halo_out[1, 2],
-        halo_out[1, 1],
-        halo_in[1, 0],
-        own(nest_e, last),
-        own(nest_n, last),
-        own(nest_n, last - 1),
-    )
-    halos[1, 0] = halo_in[1, 0]
-    halos[1, 1] = third
-    halos[1, 2] = in_grid * relax_row(
-        third, edge_row, second, e_bottom(0), n_bottom(0), own(nest_n, last)
-    )
+    receive_halo(1)
 
     for copy, guard in pending:
         if guard is None:
@@ -767,54 +832,59 @@
             pl.when(guard)(copy.wait_send)
 
 
-def finish_kernel(
-    group, start, halos, coef, parent, bulk, parent_out, nest_out, bulk_out, held, sems
-):
+GROUP = 4
+
+
+def sub_steps(start, lines, result, halos, coef):
+    values = [halves_of(start, line) for line in lines]
+    for step in range(NSUB):
+        for k, line in enumerate(lines):
+            values[k] = relax(
+                values[k],
+                halos[0, step, pl.ds(line, 1), :],
+                halos[1, step, pl.ds(line, 1), :],
+                coef,
+            )
+    for k, line in enumerate(lines):
+        for part in range(2):
+            result[line, 8 * part : 8 * part + 8] = values[k][part]
+
+
+def finish_kernel(start, halos, coef, parent, bulk, parent_out, nest_out, bulk_out, held, sems):
+    ready = pl.ds(0, HALF)
     copies = [
         pltpu.make_async_copy(parent, parent_out, sems.at[0]),
-        pltpu.make_async_copy(bulk, bulk_out, sems.at[1]),
+        pltpu.make_async_copy(start.at[ready], nest_out.at[ready], sems.at[1]),
+        pltpu.make_async_copy(bulk, bulk_out, sems.at[2]),
     ]
     for copy in copies:
         copy.start()
 
     def part_copy(at):
-        lines = pl.ds(group * at, group)
-        return pltpu.make_async_copy(held.at[lines], nest_out.at[lines], sems.at[2 + at])
+        lines = pl.ds(GROUP * at, GROUP)
+        return pltpu.make_async_copy(held.at[lines], nest_out.at[lines], sems.at[3 + at])
 
     def lines_at(at, _):
-        lines = [group * at + k for k in range(group)]
-        values = [halves_of(start, line) for line in lines]
-        for step in range(NSUB):
-            for k, line in enumerate(lines):
-                values[k] = relax(
-                    values[k],
-                    halos[0, step, pl.ds(line, 1), :],
-                    halos[1, step, pl.ds(line, 1), :],
-                    coef,
-                )
-        for k, line in enumerate(lines):
-            for part in range(2):
-                held[line, 8 * part : 8 * part + 8] = values[k][part]
+        sub_steps(start, [GROUP * at + k for k in range(GROUP)], held, halos, coef)
         part_copy(at).start()
         return 0
 
-    lax.fori_loop(0, LINES // group, lines_at, 0)
+    lax.fori_loop(HALF // GROUP, LINES // GROUP, lines_at, 0)
     for copy in copies:
         copy.wait()
-    for at in range(LINES // group):
+    for at in range(HALF // GROUP, LINES // GROUP):
         part_copy(at).wait()
 
 
 VMEM = pl.BlockSpec(memory_space=pltpu.VMEM)
 ANY = pl.BlockSpec(memory_space=pl.ANY)
-GROUP = 4
 SMEM = pl.BlockSpec(memory_space=pltpu.SMEM)
 
 
 def step_call(cap, collective, arrays):
     first = cap[0]
     grid = (LINES, ROWS, COLS)
-    copies = 3 + 1 + 20 + 8 + 2 + 2 + 4 + 2 + 3 + 2
+    copies = 3 + 1 + 28 * PARTS + 2 + 2 + 4 + 2 + 3 + 4
     shapes = [
         pltpu.VMEM(grid, F32),
         pltpu.VMEM(grid, F32),
@@ -923,7 +993,7 @@
         *arrays,
     )
     parent_adjoint, nest_adjoint, bulk_adjoint = pl.pallas_call(
-        functools.partial(finish_kernel, GROUP),
+        finish_kernel,
         out_shape=[
             jax.ShapeDtypeStruct(grid, F32),
             jax.ShapeDtypeStruct(grid, F32),
@@ -933,7 +1003,7 @@
         out_specs=[ANY] * 3,
         scratch_shapes=[
             pltpu.VMEM(grid, F32),
-            pltpu.SemaphoreType.DMA((2 + LINES // GROUP,)),
+            pltpu.SemaphoreType.DMA((3 + LINES // GROUP,)),
         ],
         compiler_params=pltpu.CompilerParams(vmem_limit_bytes=32 * 1024 * 1024),
     )(*states)

time: 52.9 us -> 49.1 us (0.928)
  Pallas kernels: 50.6 us -> 46.4 us
    pallas_call x1, Pallas kernels: 46.2 us -> 43.1 us  [step_call(): pl.pallas_call(functools.partial(step_kernel, cap), out_shape=[jax.ShapeD...]
    pallas_call x1, Pallas kernels: 2.85 us -> 1.81 us  [shards(): pl.pallas_call(finish_kernel, out_shape=[jax.ShapeDtypeStruct(grid, F32),...]
where the time goes in v4:
time: 49.1 us; the launch traced here: 48.9 us
  Pallas kernels  46.4 us (95%)
  between operations  1.49 us (3%)
  local copies, waits for them, and re-layouts  0.72 us (1%)
    pallas_call x1, Pallas kernels, step_call(): pl.pallas_call(functools.partial(step_kernel, cap), out_shape=[jax.ShapeD...  43.1 us
    pallas_call x1, Pallas kernels, shards(): pl.pallas_call(finish_kernel, out_shape=[jax.ShapeDtypeStruct(grid, F32),...  1.81 us
    pallas_call x1, Pallas kernels, shards(): pl.pallas_call(plan_kernel, out_shape=[jax.ShapeDtypeStruct((1,), jnp.int...  1.57 us

profile of v4, /device:TPU:1, one launch (start us, length us, event | category | flops | bytes accessed | tf_op | source)
XLA Modules:
  0.0 48.9 jit_solution(16176581071072490509)
XLA Ops:
  0.6 0.0 copy-start
  0.6 1.6 %shard_map.130 = (s32[1]{0:T(128)}, s32[16,256]{1,0:T(8,128)S(1)}) custom-call(s32[16,256]{1,0:T(8,128)} %tile_ref.1, s32[16]{0:T(128)} %count_ref.1), custom_call_target="tpu_custom_call" | custom-call | tf_op jit(solution)/shard_map/pallas_call | solution.py:965
  2.9 0.0 copy-done
  2.9 44.0 %conditional.1 = ((f32[16,16,1024]{2,1,0:T(8,128)S(1)}, f32[2,3,16,1024]{3,2,1,0:T(8,128)S(1)}, f32[5,16,1024]{2,1,0:T(8,128)S(1)}, f32[16,16,1024]{2,1,0:T(8,128)S(1)}, f32[8,16,256]{2,1,0:T(8,128)S(1)})) conditional(s32[]{:T(128)} %bitcast, (f32[16,16,1024]{2,1,0:T(8,128)}, f32[16,16,1024]{2,1,0:T(8,128)}, ...), branch_computations={%region_0.0_spmd, %region_1.0_spmd, %region_2.0_spmd} | conditional | bytes 65572 | solution.py:986
  2.9 0.0 copy-start.1
  2.9 0.7 %copy-done.1 = s32[16,256]{1,0:T(8,128)S(1)} copy-done((s32[16,256]{1,0:T(8,128)S(1)}, s32[16,256]{1,0:T(8,128)}, u32[]{:S(2)}) %copy-start.1) | copy-done | bytes 16408 | tf_op jit(solution)/shard_map/cond
  3.6 43.1 %branch_0_fun.1 = (f32[16,16,1024]{2,1,0:T(8,128)S(1)}, f32[2,3,16,1024]{3,2,1,0:T(8,128)S(1)}, f32[5,16,1024]{2,1,0:T(8,128)S(1)}, f32[16,16,1024]{2,1,0:T(8,128)S(1)}, f32[8,16,256]{2,1,0:T(8,128)S(1)}) custom-call(f32[16,16,1024]{2,1,0:T(8,128)} %get-tuple-element.60.parent_hbm, f32[16,16,1024]{2,1,0:T(8,128)} %get-tuple-element.61.nest_hbm, ...), custom_call_target="tpu_custom_call" | custom-call | tf_op jit(solution)/shard_map/cond/branch_0_fun/pallas_call | solution.py:932
  46.9 1.8 %shard_map.131 = (f32[16,16,1024]{2,1,0:T(8,128)}, f32[16,16,1024]{2,1,0:T(8,128)}, f32[8,16,256]{2,1,0:T(8,128)}) custom-call(f32[16,16,1024]{2,1,0:T(8,128)S(1)} %get-tuple-element.105.start, f32[2,3,16,1024]{3,2,1,0:T(8,128)S(1)} %get-tuple-element.106.halos, f32[5,16,1024]{2,1,0:T(8,128)S(1)} %get-tuple-element.107.coef, ...), custom_call_target="tpu_custom_call" | custom-call | tf_op jit(solution)/shard_map/pallas_call | solution.py:995
Async XLA Ops:
  0.6 2.2 %copy-start = (s32[16,256]{1,0:T(8,128)S(1)}, s32[16,256]{1,0:T(8,128)}, u32[]{:S(2)}) copy-start(s32[16,256]{1,0:T(8,128)} %param.22) | copy-start | bytes 49156
  2.9 0.7 %copy-start.1 = (s32[16,256]{1,0:T(8,128)S(1)}, s32[16,256]{1,0:T(8,128)}, u32[]{:S(2)}) copy-start(s32[16,256]{1,0:T(8,128)} %get-tuple-element.68.target_hbm) | copy-start | bytes 49156 | tf_op jit(solution)/shard_map/cond
